TPU v7x, 32 devices: a whole 2x2x4 slice. The times are simulated.
32 devices in a mesh: fsdp: 8 (over y, x, core), rep: 4 (over z).
Axes of the slice: x: 2, y: 2, z: 4, core: 2. Of those that a mesh axis runs over, the one named last changes fastest.
Arguments:
- tokens_in: bfloat16 [2, 64, 256, 768], P(None, ('fsdp', 'rep')), may hold values from -6 to 6
- image_sizes: int32 [2, 64, 2], P(None, ('fsdp', 'rep')), may hold values from 1 to 17, as said below
- gain_one: bfloat16 [768], P('fsdp'), may hold values from 0.25 to 1.75
- shift_one: bfloat16 [768], P('fsdp'), may hold values from -3 to 3
- project_in: bfloat16 [768, 2304], P('fsdp'), may hold values from -0.21875 to 0.21875
- query_bias: bfloat16 [768], P('fsdp'), may hold values from -4 to 4
- value_bias: bfloat16 [768], P('fsdp'), may hold values from -4 to 4
- bias_table: bfloat16 [960, 12], P('fsdp'), may hold values from -4 to 4
- project_out: bfloat16 [768, 768], P('fsdp'), may hold values from -1.75 to 1.75
- out_bias: bfloat16 [768], P('fsdp'), may hold values from -3 to 3
- scale_one: bfloat16 [768], P('fsdp'), may hold values from 0.29882812 to 1.5
- gain_two: bfloat16 [768], P('fsdp'), may hold values from 0.25 to 1.75
- shift_two: bfloat16 [768], P('fsdp'), may hold values from -3 to 3
- expand_weight: bfloat16 [768, 3072], P('fsdp'), may hold values from -0.21875 to 0.21875
- expand_bias: bfloat16 [3072], P('fsdp'), may hold values from -4 to 4
- reduce_weight: bfloat16 [3072, 768], P('fsdp'), may hold values from -0.21875 to 0.21875
- reduce_bias: bfloat16 [768], P('fsdp'), may hold values from -3 to 3
- scale_two: bfloat16 [768], P('fsdp'), may hold values from 0.29882812 to 1.5
- cotangent: bfloat16 [2, 64, 256, 768], P(None, ('fsdp', 'rep')), may hold values from -6 to 6
Outputs:
- block_out: bfloat16 [2, 64, 256, 768], P(None, ('fsdp', 'rep'))
- input_grad: bfloat16 [2, 64, 256, 768], P(None, ('fsdp', 'rep'))
- grad_gain_one: float32 [768], P('fsdp')
- grad_shift_one: float32 [768], P('fsdp')
- grad_project_in: float32 [768, 2304], P('fsdp')
- grad_query_bias: float32 [768], P('fsdp')
- grad_value_bias: float32 [768], P('fsdp')
- grad_bias_table: float32 [960, 12], P('fsdp')
- grad_project_out: float32 [768, 768], P('fsdp')
- grad_out_bias: float32 [768], P('fsdp')
- grad_scale_one: float32 [768], P('fsdp')
- grad_gain_two: float32 [768], P('fsdp')
- grad_shift_two: float32 [768], P('fsdp')
- grad_expand_weight: float32 [768, 3072], P('fsdp')
- grad_expand_bias: float32 [3072], P('fsdp')
- grad_reduce_weight: float32 [3072, 768], P('fsdp')
- grad_reduce_bias: float32 [768], P('fsdp')
- grad_scale_two: float32 [768], P('fsdp')
Inputs may be any that keep to these rules, and one draw needn't show every extreme that they name: image_sizes[m, i] holds the height (1 to 15) and the width (1 to 17) of image i of micro-batch m; its 1 + height * width tokens fill the first of its 256 slots, the class token first and then the patches row by row, the rest is padding; in every micro-batch some image is 15 by 17.
All inputs are finite; a program needn't handle non-finite values.
Results may differ from a plain program's by a relative error of at most 0.015.
Values may be sent and summed in bfloat16 or wider, within the bound.
No kernel may reach another device: no remote copies, remote signals or barrier semaphores. Data moves between devices by JAX's collectives and lax.ppermute only.
A program may use at most 192 MiB of HBM per device.

v0:
```python
import jax
import jax.numpy as jnp
from jax import lax
from jax.sharding import PartitionSpec as P

GH = 15
GW = 17
NREL = 960


epsilon = 1e-06
negative = -1000000000.0
inv_root_two = 0.7071067811865476
inv_root_tau = 0.3989422804014327


def grid_index(first_pos, second_pos):
    first_off = jnp.maximum(first_pos - 1, 0)
    second_off = jnp.maximum(second_pos - 1, 0)
    row_offset = first_off // GW - second_off // GW + GH - 1
    column_offset = first_off % GW - second_off % GW + GW - 1
    inner = row_offset * (2 * GW - 1) + column_offset
    first_zero = first_pos == 0
    second_zero = second_pos == 0
    return jnp.where(
        first_zero & second_zero,
        NREL - 1,
        jnp.where(first_zero, NREL - 3, jnp.where(second_zero, NREL - 2, inner)),
    )


def block_rows(size_s, limit):
    chosen = 1
    for candidate in range(1, size_s + 1):
        if size_s % candidate == 0 and candidate * size_s <= limit:
            chosen = candidate
    return chosen


def build_tiles(table_full, size_s):
    rows = block_rows(size_s, 16384)
    heads_count = table_full.shape[1]
    table_cols = table_full.T

    def build_one_block(start):
        first_pos = start + jnp.arange(rows)
        index = grid_index(first_pos[:, None], jnp.arange(size_s)[None, :]).reshape(-1)
        onehot = (jnp.arange(NREL)[:, None] == index[None, :]).astype(jnp.bfloat16)
        return jnp.dot(table_cols, onehot, preferred_element_type=jnp.float32)

    blocks = lax.map(build_one_block, jnp.arange(0, size_s, rows))
    blocks = blocks.reshape(size_s // rows, heads_count, rows, size_s)
    return (
        jnp.transpose(blocks, (1, 0, 2, 3))
        .reshape(heads_count, size_s, size_s)
        .astype(jnp.bfloat16)
    )


def table_grad(tile_grads, size_s):
    rows = block_rows(size_s, 16384)
    heads_count = tile_grads.shape[0]
    blocked = tile_grads.reshape(heads_count, size_s // rows, rows * size_s)
    blocked = jnp.transpose(blocked, (1, 0, 2))

    def table_one_block(paired):
        start, piece = paired
        first_pos = start + jnp.arange(rows)
        index = grid_index(first_pos[:, None], jnp.arange(size_s)[None, :]).reshape(-1)
        onehot = (index[:, None] == jnp.arange(NREL)[None, :]).astype(jnp.bfloat16)
        high_part = piece.astype(jnp.bfloat16)
        low_part = (piece - high_part.astype(jnp.float32)).astype(jnp.bfloat16)
        return jnp.dot(high_part, onehot, preferred_element_type=jnp.float32) + jnp.dot(
            low_part, onehot, preferred_element_type=jnp.float32
        )

    pieces = lax.map(table_one_block, (jnp.arange(0, size_s, rows), blocked))
    return jnp.sum(pieces, axis=0).T


def token_places(sizes, size_s):
    heights = sizes[:, 0:1]
    widths = sizes[:, 1:2]
    slots = jnp.arange(size_s)[None, :]
    valid = slots < 1 + heights * widths
    offset = jnp.maximum(slots - 1, 0)
    spot = 1 + offset // widths * GW + offset % widths
    spot = jnp.where(slots == 0, 0, spot)
    spot = jnp.where(valid, spot, -1)
    places = (spot[:, :, None] == jnp.arange(size_s)[None, None, :]).astype(jnp.bfloat16)
    return (valid, places)


def normalize(values, gain, shift):
    center = values - jnp.mean(values, axis=-1, keepdims=True)
    inverse = lax.rsqrt(jnp.mean(center * center, axis=-1, keepdims=True) + epsilon)
    unit = center * inverse
    return (unit * gain + shift, unit, inverse)


def normalize_back(grad_out, unit, inverse, gain):
    scaled = grad_out * gain
    return inverse * (
        scaled
        - jnp.mean(scaled, axis=-1, keepdims=True)
        - unit * jnp.mean(scaled * unit, axis=-1, keepdims=True)
    )


def dot_rows(left, right):
    return lax.dot_general(
        left, right, (((0,), (0,)), ((), ())), preferred_element_type=jnp.float32
    )


def dot_trans(left, right):
    return lax.dot_general(
        left, right, (((1,), (1,)), ((), ())), preferred_element_type=jnp.float32
    )


def column_sum(values):
    return jnp.sum(values.astype(jnp.float32), axis=0)


def add_trees(first, second):
    return jax.tree.map(lambda one, two: one + two, first, second)


def shards(
    tokens_in,
    image_sizes,
    gain_one,
    shift_one,
    project_in,
    query_bias,
    value_bias,
    bias_table,
    project_out,
    out_bias,
    scale_one,
    gain_two,
    shift_two,
    expand_weight,
    expand_bias,
    reduce_weight,
    reduce_bias,
    scale_two,
    cotangent,
):
    batches, images, size_s, width = tokens_in.shape
    heads_count = bias_table.shape[1]
    head_size = width // heads_count
    rows = images * size_s
    outputs = []
    in_grads = []
    summed = None
    tile_total = jnp.zeros((heads_count, size_s, size_s), jnp.float32)
    for batch in range(batches):
        current = (
            lax.all_gather(gain_one, "fsdp", axis=0, tiled=True),
            lax.all_gather(shift_one, "fsdp", axis=0, tiled=True),
            lax.all_gather(project_in, "fsdp", axis=0, tiled=True),
            lax.all_gather(query_bias, "fsdp", axis=0, tiled=True),
            lax.all_gather(value_bias, "fsdp", axis=0, tiled=True),
            lax.all_gather(bias_table, "fsdp", axis=0, tiled=True),
            lax.all_gather(project_out, "fsdp", axis=0, tiled=True),
            lax.all_gather(out_bias, "fsdp", axis=0, tiled=True),
            lax.all_gather(scale_one, "fsdp", axis=0, tiled=True),
            lax.all_gather(gain_two, "fsdp", axis=0, tiled=True),
            lax.all_gather(shift_two, "fsdp", axis=0, tiled=True),
            lax.all_gather(expand_weight, "fsdp", axis=0, tiled=True),
            lax.all_gather(expand_bias, "fsdp", axis=0, tiled=True),
            lax.all_gather(reduce_weight, "fsdp", axis=0, tiled=True),
            lax.all_gather(reduce_bias, "fsdp", axis=0, tiled=True),
            lax.all_gather(scale_two, "fsdp", axis=0, tiled=True),
        )
        norm_gain = current[0].astype(jnp.float32)
        norm_shift = current[1].astype(jnp.float32)
        inner_weight = current[2]
        query_add = current[3].astype(jnp.float32)
        value_add = current[4].astype(jnp.float32)
        table_full = current[5]
        outer_weight = current[6]
        outer_add = current[7].astype(jnp.float32)
        layer_scale = current[8].astype(jnp.float32)
        second_gain = current[9].astype(jnp.float32)
        second_shift = current[10].astype(jnp.float32)
        expand_full = current[11]
        expand_add = current[12].astype(jnp.float32)
        reduce_full = current[13]
        reduce_add = current[14].astype(jnp.float32)
        final_scale = current[15].astype(jnp.float32)
        tiles = build_tiles(table_full, size_s)
        valid, places = token_places(image_sizes[batch], size_s)
        left_part = jnp.einsum(
            "itp,hpq->ihtq", places, tiles, preferred_element_type=jnp.float32
        ).astype(jnp.bfloat16)
        relative = jnp.einsum(
            "ihtq,isq->ihts", left_part, places, preferred_element_type=jnp.float32
        )
        addend = jnp.where(valid[:, None, None, :], relative, negative)
        inputs = tokens_in[batch].reshape(rows, width).astype(jnp.float32)
        normed, unit_one, inverse_one = normalize(inputs, norm_gain, norm_shift)
        act_one = normed.astype(jnp.bfloat16)
        mixed = jnp.dot(act_one, inner_weight, preferred_element_type=jnp.float32)
        query = (
            ((mixed[:, :width] + query_add) * 0.125)
            .astype(jnp.bfloat16)
            .reshape(images, size_s, heads_count, head_size)
        )
        keys = (
            mixed[:, width : 2 * width]
            .astype(jnp.bfloat16)
            .reshape(images, size_s, heads_count, head_size)
        )
        values = (
            (mixed[:, 2 * width :] + value_add)
            .astype(jnp.bfloat16)
            .reshape(images, size_s, heads_count, head_size)
        )
        scores = (
            jnp.einsum("ishd,ithd->ihst", query, keys, preferred_element_type=jnp.float32) + addend
        )
        peak = jnp.max(scores, axis=-1, keepdims=True)
        exponent = jnp.exp(scores - peak)
        total = jnp.sum(exponent, axis=-1, keepdims=True)
        probs = exponent / total
        log_total = peak + jnp.log(total)
        heads = jnp.einsum(
            "ihst,ithd->ishd",
            probs.astype(jnp.bfloat16),
            values,
            preferred_element_type=jnp.float32,
        )
        heads = heads.reshape(rows, width).astype(jnp.bfloat16)
        attended = jnp.dot(heads, outer_weight, preferred_element_type=jnp.float32) + outer_add
        middle = inputs + layer_scale * attended
        normed_two, unit_two, inverse_two = normalize(middle, second_gain, second_shift)
        act_two = normed_two.astype(jnp.bfloat16)
        hidden = jnp.dot(act_two, expand_full, preferred_element_type=jnp.float32) + expand_add
        active = jax.nn.gelu(hidden, approximate=False).astype(jnp.bfloat16)
        down = jnp.dot(active, reduce_full, preferred_element_type=jnp.float32) + reduce_add
        result = middle + final_scale * down
        outputs.append(result.astype(jnp.bfloat16).reshape(images, size_s, width))
        back_set = (
            lax.all_gather(gain_one, "fsdp", axis=0, tiled=True),
            lax.all_gather(project_in, "fsdp", axis=0, tiled=True),
            lax.all_gather(project_out, "fsdp", axis=0, tiled=True),
            lax.all_gather(scale_one, "fsdp", axis=0, tiled=True),
            lax.all_gather(gain_two, "fsdp", axis=0, tiled=True),
            lax.all_gather(expand_weight, "fsdp", axis=0, tiled=True),
            lax.all_gather(reduce_weight, "fsdp", axis=0, tiled=True),
            lax.all_gather(scale_two, "fsdp", axis=0, tiled=True),
        )
        back_gain = back_set[0].astype(jnp.float32)
        back_inner = back_set[1]
        back_outer = back_set[2]
        back_scale = back_set[3].astype(jnp.float32)
        back_gain_two = back_set[4].astype(jnp.float32)
        back_expand = back_set[5]
        back_reduce = back_set[6]
        back_final = back_set[7].astype(jnp.float32)
        upstream = cotangent[batch].reshape(rows, width).astype(jnp.float32)
        grad_final = jnp.sum(upstream * down, axis=0)
        d_down = (back_final * upstream).astype(jnp.bfloat16)
        grad_reduce_add = column_sum(d_down)
        grad_reduce = dot_rows(active, d_down)
        d_active = dot_trans(d_down, back_reduce)
        normal_cdf = 0.5 * (1.0 + lax.erf(hidden * inv_root_two))
        slope = normal_cdf + hidden * jnp.exp(-0.5 * hidden * hidden) * inv_root_tau
        d_hidden = (d_active * slope).astype(jnp.bfloat16)
        grad_expand_add = column_sum(d_hidden)
        grad_expand = dot_rows(act_two, d_hidden)
        d_act_two = dot_trans(d_hidden, back_expand)
        grad_gain_two = jnp.sum(d_act_two * unit_two, axis=0)
        grad_shift_two = jnp.sum(d_act_two, axis=0)
        d_middle = upstream + normalize_back(d_act_two, unit_two, inverse_two, back_gain_two)
        grad_scale = jnp.sum(d_middle * attended, axis=0)
        d_attended = (back_scale * d_middle).astype(jnp.bfloat16)
        grad_outer_add = column_sum(d_attended)
        grad_outer = dot_rows(heads, d_attended)
        d_heads = (
            dot_trans(d_attended, back_outer)
            .astype(jnp.bfloat16)
            .reshape(images, size_s, heads_count, head_size)
        )
        scores_again = (
            jnp.einsum("ishd,ithd->ihst", query, keys, preferred_element_type=jnp.float32) + addend
        )
        probs_again = jnp.exp(scores_again - log_total)
        d_probs = jnp.einsum("ishd,ithd->ihst", d_heads, values, preferred_element_type=jnp.float32)
        inner_sum = jnp.sum(d_probs * probs_again, axis=-1, keepdims=True)
        d_scores = (probs_again * (d_probs - inner_sum)).astype(jnp.bfloat16)
        d_values = jnp.einsum(
            "ihst,ishd->ithd",
            probs_again.astype(jnp.bfloat16),
            d_heads,
            preferred_element_type=jnp.float32,
        ).astype(jnp.bfloat16)
        d_query = jnp.einsum(
            "ihst,ithd->ishd", d_scores, keys, preferred_element_type=jnp.float32
        ).astype(jnp.bfloat16)
        d_keys = jnp.einsum(
            "ihst,ishd->ithd", d_scores, query, preferred_element_type=jnp.float32
        ).astype(jnp.bfloat16)
        left_grad = jnp.einsum(
            "itp,ihts->ihps", places, d_scores, preferred_element_type=jnp.float32
        ).astype(jnp.bfloat16)
        tile_batch = jnp.einsum(
            "ihps,isq->hpq", left_grad, places, preferred_element_type=jnp.float32
        )
        query_part = d_query.reshape(rows, width) * 0.125
        value_part = d_values.reshape(rows, width)
        d_mixed = jnp.concatenate([query_part, d_keys.reshape(rows, width), value_part], axis=1)
        grad_query_add = column_sum(query_part)
        grad_value_add = column_sum(value_part)
        grad_inner = dot_rows(act_one, d_mixed)
        d_act_one = dot_trans(d_mixed, back_inner)
        grad_gain_one = jnp.sum(d_act_one * unit_one, axis=0)
        grad_shift_one = jnp.sum(d_act_one, axis=0)
        d_inputs = d_middle + normalize_back(d_act_one, unit_one, inverse_one, back_gain)
        in_grads.append(d_inputs.astype(jnp.bfloat16).reshape(images, size_s, width))
        tile_total = tile_total + tile_batch
        batch_grads = (
            grad_gain_one,
            grad_shift_one,
            grad_inner,
            grad_query_add,
            grad_value_add,
            grad_outer,
            grad_outer_add,
            grad_scale,
            grad_gain_two,
            grad_shift_two,
            grad_expand,
            grad_expand_add,
            grad_reduce,
            grad_reduce_add,
            grad_final,
        )
        summed = batch_grads if summed is None else add_trees(summed, batch_grads)
    table_whole = table_grad(tile_total, size_s)
    summed = (
        lax.psum_scatter(summed[0], "fsdp", scatter_dimension=0, tiled=True),
        lax.psum_scatter(summed[1], "fsdp", scatter_dimension=0, tiled=True),
        lax.psum_scatter(summed[2], "fsdp", scatter_dimension=0, tiled=True),
        lax.psum_scatter(summed[3], "fsdp", scatter_dimension=0, tiled=True),
        lax.psum_scatter(summed[4], "fsdp", scatter_dimension=0, tiled=True),
        lax.psum_scatter(table_whole, "fsdp", scatter_dimension=0, tiled=True),
        lax.psum_scatter(summed[5], "fsdp", scatter_dimension=0, tiled=True),
        lax.psum_scatter(summed[6], "fsdp", scatter_dimension=0, tiled=True),
        lax.psum_scatter(summed[7], "fsdp", scatter_dimension=0, tiled=True),
        lax.psum_scatter(summed[8], "fsdp", scatter_dimension=0, tiled=True),
        lax.psum_scatter(summed[9], "fsdp", scatter_dimension=0, tiled=True),
        lax.psum_scatter(summed[10], "fsdp", scatter_dimension=0, tiled=True),
        lax.psum_scatter(summed[11], "fsdp", scatter_dimension=0, tiled=True),
        lax.psum_scatter(summed[12], "fsdp", scatter_dimension=0, tiled=True),
        lax.psum_scatter(summed[13], "fsdp", scatter_dimension=0, tiled=True),
        lax.psum_scatter(summed[14], "fsdp", scatter_dimension=0, tiled=True),
    )
    totals = (
        lax.psum(summed[0].astype(jnp.bfloat16), "rep").astype(jnp.float32),
        lax.psum(summed[1].astype(jnp.bfloat16), "rep").astype(jnp.float32),
        lax.psum(summed[2].astype(jnp.bfloat16), "rep").astype(jnp.float32),
        lax.psum(summed[3].astype(jnp.bfloat16), "rep").astype(jnp.float32),
        lax.psum(summed[4].astype(jnp.bfloat16), "rep").astype(jnp.float32),
        lax.psum(summed[5].astype(jnp.bfloat16), "rep").astype(jnp.float32),
        lax.psum(summed[6].astype(jnp.bfloat16), "rep").astype(jnp.float32),
        lax.psum(summed[7].astype(jnp.bfloat16), "rep").astype(jnp.float32),
        lax.psum(summed[8].astype(jnp.bfloat16), "rep").astype(jnp.float32),
        lax.psum(summed[9].astype(jnp.bfloat16), "rep").astype(jnp.float32),
        lax.psum(summed[10].astype(jnp.bfloat16), "rep").astype(jnp.float32),
        lax.psum(summed[11].astype(jnp.bfloat16), "rep").astype(jnp.float32),
        lax.psum(summed[12].astype(jnp.bfloat16), "rep").astype(jnp.float32),
        lax.psum(summed[13].astype(jnp.bfloat16), "rep").astype(jnp.float32),
        lax.psum(summed[14].astype(jnp.bfloat16), "rep").astype(jnp.float32),
        lax.psum(summed[15].astype(jnp.bfloat16), "rep").astype(jnp.float32),
    )
    return (
        jnp.stack(outputs),
        jnp.stack(in_grads),
        totals[0],
        totals[1],
        totals[2],
        totals[3],
        totals[4],
        totals[5],
        totals[6],
        totals[7],
        totals[8],
        totals[9],
        totals[10],
        totals[11],
        totals[12],
        totals[13],
        totals[14],
        totals[15],
    )


def solution(mesh):
    placed = (
        P(None, ("fsdp", "rep"), None, None),
        P(None, ("fsdp", "rep"), None),
        P("fsdp"),
        P("fsdp"),
        P("fsdp", None),
        P("fsdp"),
        P("fsdp"),
        P("fsdp", None),
        P("fsdp", None),
        P("fsdp"),
        P("fsdp"),
        P("fsdp"),
        P("fsdp"),
        P("fsdp", None),
        P("fsdp"),
        P("fsdp", None),
        P("fsdp"),
        P("fsdp"),
        P(None, ("fsdp", "rep"), None, None),
    )
    return jax.shard_map(
        shards,
        mesh=mesh,
        in_specs=placed,
        out_specs=(
            P(None, ("fsdp", "rep"), None, None),
            P(None, ("fsdp", "rep"), None, None),
            P("fsdp"),
            P("fsdp"),
            P("fsdp", None),
            P("fsdp"),
            P("fsdp"),
            P("fsdp", None),
            P("fsdp", None),
            P("fsdp"),
            P("fsdp"),
            P("fsdp"),
            P("fsdp"),
            P("fsdp", None),
            P("fsdp"),
            P("fsdp", None),
            P("fsdp"),
            P("fsdp"),
        ),
        check_vma=False,
    )
```

profile of v0, /device:TPU:0, one launch (start us, length us, event | category | flops | bytes accessed | tf_op | source)
XLA Modules:
  0.0 696.9 jit_solution(5413180996279693788)
XLA Ops:
  22.4 25.8 %all-reduce.23 = (bf16[768]{0:T(1024)(128)(2,1)S(1)}, bf16[768]{0:T(1024)(128)(2,1)S(1)}, bf16[768]{0:T(1024)(128)(2,1)S(1)}, bf16[768]{0:T(1024)(128)(2,1)S(1)}...) all-reduce(bf16[768]{0:T(1024)(128)(2,1)S(1)} %dynamic-update-slice, ...), channel_id=1, replica_groups=mesh['fsdp'=8,'rep'=4] {'fsdp'}, use_global_device_ids=true, to_apply=%add.2 | all-reduce | flops 7680 | bytes 30720
  51.4 8.0 %all-gather.1 = bf16[8,1,384]{2,1,0:T(2,128)(2,1)S(1)} all-gather(bf16[1,1,384]{2,1,0:T(2,128)(2,1)S(1)} %reshape.777), channel_id=1, replica_groups=mesh['fsdp'=8,'rep'=4] {'fsdp'}, dimensions={0}, use_global_device_ids=true | all-gather | bytes 6912 | tf_op jit(solution)/shard_map/all_gather | solution.py:173
  59.4 9.0 %all-gather = bf16[8,120,12]{1,2,0:T(8,128)(2,1)S(1)} all-gather(bf16[1,120,12]{1,2,0:T(8,128)(2,1)S(1)} %bitcast.398), channel_id=1, replica_groups=mesh['fsdp'=8,'rep'=4] {'fsdp'}, dimensions={0}, use_global_device_ids=true | all-gather | bytes 25920 | tf_op jit(solution)/shard_map/all_gather | solution.py:166
  68.5 51.3 %while.34 = (s32[]{:T(128)}, bf16[4,12,16384]{2,1,0:T(8,128)(2,1)}, s32[4]{0:T(128)S(1)}, bf16[12,960]{1,0:T(8,128)(2,1)S(1)}, s32[]{:T(128)}) while((s32[]{:T(128)}, bf16[4,12,16384]{2,1,0:T(8,128)(2,1)}, s32[4]{0:T(128)S(1)}, bf16[12,960]{1,0:T(8,128)(2,1)S(1)}, s32[]{:T(128)}) %tuple.187), condition=%wide.region_3.4_spmd, body=%wide.region_2.3_spmd.sunk | while | flops 393384768 | bytes 1601757 | solution.py:51
  71.3 10.4 %fusion.297 = bf16[4,12,16384]{2,1,0:T(8,128)(2,1)} fusion(bf16[4,12,16384]{2,1,0:T(8,128)(2,1)} %get-tuple-element.498, s32[]{:T(128)S(6)} %copy.377, bf16[12,960]{1,0:T(8,128)(2,1)S(1)} %get-tuple-element.505, s32[16384]{0:T(1024)S(1)} %select_select_fusion.4), kind=kOutput, calls=%fused_computation.4.clone.1 | convolution fusion | flops 393216000 | bytes 1137156 | tf_op jit(solution)/shard_map/while/body/eval_jaxpr/dot_general | solution.py:49
  84.0 10.4 %fusion.297 = bf16[4,12,16384]{2,1,0:T(8,128)(2,1)} fusion(bf16[4,12,16384]{2,1,0:T(8,128)(2,1)} %get-tuple-element.498, s32[]{:T(128)S(6)} %copy.377, bf16[12,960]{1,0:T(8,128)(2,1)S(1)} %get-tuple-element.505, s32[16384]{0:T(1024)S(1)} %select_select_fusion.4), kind=kOutput, calls=%fused_computation.4.clone.1 | convolution fusion | flops 393216000 | bytes 1137156 | tf_op jit(solution)/shard_map/while/body/eval_jaxpr/dot_general | solution.py:49
  96.7 10.4 %fusion.297 = bf16[4,12,16384]{2,1,0:T(8,128)(2,1)} fusion(bf16[4,12,16384]{2,1,0:T(8,128)(2,1)} %get-tuple-element.498, s32[]{:T(128)S(6)} %copy.377, bf16[12,960]{1,0:T(8,128)(2,1)S(1)} %get-tuple-element.505, s32[16384]{0:T(1024)S(1)} %select_select_fusion.4), kind=kOutput, calls=%fused_computation.4.clone.1 | convolution fusion | flops 393216000 | bytes 1137156 | tf_op jit(solution)/shard_map/while/body/eval_jaxpr/dot_general | solution.py:49
  109.4 10.4 %fusion.297 = bf16[4,12,16384]{2,1,0:T(8,128)(2,1)} fusion(bf16[4,12,16384]{2,1,0:T(8,128)(2,1)} %get-tuple-element.498, s32[]{:T(128)S(6)} %copy.377, bf16[12,960]{1,0:T(8,128)(2,1)S(1)} %get-tuple-element.505, s32[16384]{0:T(1024)S(1)} %select_select_fusion.4), kind=kOutput, calls=%fused_computation.4.clone.1 | convolution fusion | flops 393216000 | bytes 1137156 | tf_op jit(solution)/shard_map/while/body/eval_jaxpr/dot_general | solution.py:49
  184.6 7.1 %fusion.224 = (f32[2,12,256]{2,1,0:T(8,128)S(1)}, f32[2,12,256,256]{2,3,1,0:T(8,128)}) fusion(f32[2,12,256,256]{2,3,1,0:T(8,128)} %fusion.179, s32[2,256]{1,0:T(2,128)S(1)} %get-tuple-element.383, bf16[12,256,256,1]{2,1,0,3:T(8,128)(2,1)S(1)} %bitcast.352, pred[2,256]{1,0:T(4,128)(4,1)S(1)} %iota_compare_fusion.20), kind=kOutput, calls=%fused_computation.366 | convolution fusion | flops 1617160192 | bytes 14182912 | tf_op jit(solution)/shard_map/ihtq,isq->ihts/dot_general | solution.py:199
  204.2 7.0 fusion.227
  233.4 31.1 %fusion.23 = (bf16[512,3072]{1,0:T(8,128)(2,1)}, bf16[512,3072]{1,0:T(8,128)(2,1)}, f32[512,3072]{1,0:T(8,128)}) fusion(f32[3072]{0:T(1024)S(1)} %bitcast.395, f32[512,3072]{1,0:T(8,128)S(1)} %fusion.220, bf16[768,3072]{1,0:T(8,128)(2,1)S(1)} %copy-done.78, f32[512,768]{1,0:T(8,128)S(1)} %copy-done.24, f32[768]{0:T(1024)S(1)} %convert_element_type.462, ...), kind=kOutput, calls=%fused_computation.50 | convolution fusion | flops 2625503232 | bytes 25188352 | tf_op jit(solution)/shard_map/dot_general | solution.py:241
  264.5 7.6 %convert_reduce_fusion.1 = (f32[3072]{0:T(1024)S(1)}, bf16[512,3072]{1,0:T(8,128)(2,1)S(1)}) fusion(f32[512,3072]{1,0:T(8,128)} %get-tuple-element.398, f32[3072]{0:T(1024)S(1)} %bitcast.396, bf16[512,768]{1,0:T(8,128)(2,1)} %fusion.111, bf16[3072,768]{1,0:T(8,128)(2,1)} %all-gather.13.cloned.1.call-done), kind=kOutput, calls=%fused_computation.67 | convolution fusion | flops 2436363264 | bytes 14966784 | tf_op jit(solution)/shard_map/dot_general | solution.py:117
  281.0 5.8 fusion.109
  305.1 7.0 %multiply_reduce_fusion = (f32[2,12,256]{2,1,0:T(8,128)S(1)}, f32[2,12,256,256]{2,3,1,0:T(8,128)}) fusion(f32[2,12,256,256]{2,3,1,0:T(8,128)} %get-tuple-element.396, f32[2,12,256]{2,1,0:T(8,128)S(1)} %log_add_fusion, bf16[2,256,12,64]{1,0,3,2:T(2,128)(2,1)S(1)} %copy-done.37, bf16[2,256,12,64]{1,0,3,2:T(2,128)(2,1)S(1)} %reshape.737), kind=kOutput, calls=%fused_computation.69 | convolution fusion | flops 206039040 | bytes 14204928 | tf_op jit(solution)/shard_map/ishd,ithd->ihst/dot_general | solution.py:292
  320.4 7.0 %multiply_reduce_fusion.1 = (f32[2,12,256]{2,1,0:T(8,128)S(1)}, f32[2,12,256,256]{2,3,1,0:T(8,128)}) fusion(f32[2,12,256,256]{2,3,1,0:T(8,128)} %get-tuple-element.394, f32[2,12,256]{2,1,0:T(8,128)S(1)} %copy-done.59, bf16[2,256,12,64]{1,0,3,2:T(2,128)(2,1)S(1)} %copy-done.36, bf16[2,256,12,64]{1,0,3,2:T(2,128)(2,1)S(1)} %reshape.734), kind=kOutput, calls=%fused_computation.72 | convolution fusion | flops 206039040 | bytes 14204928 | tf_op jit(solution)/shard_map/ishd,ithd->ihst/dot_general | solution.py:292
  333.9 6.9 multiply_convert_fusion
  370.7 5.8 convolution_add_fusion.2
  381.8 6.4 convolution_add_fusion.1
  396.9 6.9 bitcast_add_fusion
  411.6 107.7 %while.35 = (s32[]{:T(128)}, f32[4,12,960]{2,1,0:T(8,128)S(1)}, f32[4,12,16384]{2,1,0:T(8,128)}, s32[4]{0:T(128)S(1)}, s32[]{:T(128)}) while((s32[]{:T(128)}, f32[4,12,960]{2,1,0:T(8,128)S(1)}, f32[4,12,16384]{2,1,0:T(8,128)}, s32[4]{0:T(128)S(1)}, s32[]{:T(128)}) %tuple.188), condition=%wide.region_43.46_spmd, body=%wide.region_42.45_spmd.sunk | while | flops 787398720 | bytes 2346717 | solution.py:77
  413.8 12.3 %fusion.300 = f32[12,960]{1,0:T(8,128)S(1)} fusion(s32[16384]{0:T(1024)S(1)} %select_select_fusion.5, f32[4,12,16384]{2,1,0:T(8,128)} %get-tuple-element.519, s32[]{:T(128)S(6)} %copy.387), kind=kOutput, calls=%fused_computation.19.clone.1 | convolution fusion | flops 394002432 | bytes 1160196 | tf_op jit(solution)/shard_map/while/body/eval_jaxpr/dot_general | solution.py:73
  426.1 12.3 %fusion.301 = f32[4,12,960]{2,1,0:T(8,128)S(1)} fusion(f32[4,12,960]{2,1,0:T(8,128)S(1)} %get-tuple-element.513, s32[]{:T(128)S(6)} %copy.387, f32[12,960]{1,0:T(8,128)S(1)} %fusion.300, s32[16384]{0:T(1024)S(1)} %select_select_fusion.5, f32[4,12,16384]{2,1,0:T(8,128)} %get-tuple-element.519), kind=kOutput, calls=%fused_computation.25.clone.1 | convolution fusion | flops 393227520 | bytes 721920 | tf_op jit(solution)/shard_map/while/body/eval_jaxpr/dot_general | solution.py:73
  440.7 12.3 %fusion.300 = f32[12,960]{1,0:T(8,128)S(1)} fusion(s32[16384]{0:T(1024)S(1)} %select_select_fusion.5, f32[4,12,16384]{2,1,0:T(8,128)} %get-tuple-element.519, s32[]{:T(128)S(6)} %copy.387), kind=kOutput, calls=%fused_computation.19.clone.1 | convolution fusion | flops 394002432 | bytes 1160196 | tf_op jit(solution)/shard_map/while/body/eval_jaxpr/dot_general | solution.py:73
  452.9 12.4 %fusion.301 = f32[4,12,960]{2,1,0:T(8,128)S(1)} fusion(f32[4,12,960]{2,1,0:T(8,128)S(1)} %get-tuple-element.513, s32[]{:T(128)S(6)} %copy.387, f32[12,960]{1,0:T(8,128)S(1)} %fusion.300, s32[16384]{0:T(1024)S(1)} %select_select_fusion.5, f32[4,12,16384]{2,1,0:T(8,128)} %get-tuple-element.519), kind=kOutput, calls=%fused_computation.25.clone.1 | convolution fusion | flops 393227520 | bytes 721920 | tf_op jit(solution)/shard_map/while/body/eval_jaxpr/dot_general | solution.py:73
  467.6 12.3 %fusion.300 = f32[12,960]{1,0:T(8,128)S(1)} fusion(s32[16384]{0:T(1024)S(1)} %select_select_fusion.5, f32[4,12,16384]{2,1,0:T(8,128)} %get-tuple-element.519, s32[]{:T(128)S(6)} %copy.387), kind=kOutput, calls=%fused_computation.19.clone.1 | convolution fusion | flops 394002432 | bytes 1160196 | tf_op jit(solution)/shard_map/while/body/eval_jaxpr/dot_general | solution.py:73
  479.9 12.3 %fusion.301 = f32[4,12,960]{2,1,0:T(8,128)S(1)} fusion(f32[4,12,960]{2,1,0:T(8,128)S(1)} %get-tuple-element.513, s32[]{:T(128)S(6)} %copy.387, f32[12,960]{1,0:T(8,128)S(1)} %fusion.300, s32[16384]{0:T(1024)S(1)} %select_select_fusion.5, f32[4,12,16384]{2,1,0:T(8,128)} %get-tuple-element.519), kind=kOutput, calls=%fused_computation.25.clone.1 | convolution fusion | flops 393227520 | bytes 721920 | tf_op jit(solution)/shard_map/while/body/eval_jaxpr/dot_general | solution.py:73
  494.4 12.3 %fusion.300 = f32[12,960]{1,0:T(8,128)S(1)} fusion(s32[16384]{0:T(1024)S(1)} %select_select_fusion.5, f32[4,12,16384]{2,1,0:T(8,128)} %get-tuple-element.519, s32[]{:T(128)S(6)} %copy.387), kind=kOutput, calls=%fused_computation.19.clone.1 | convolution fusion | flops 394002432 | bytes 1160196 | tf_op jit(solution)/shard_map/while/body/eval_jaxpr/dot_general | solution.py:73
  506.7 12.3 %fusion.301 = f32[4,12,960]{2,1,0:T(8,128)S(1)} fusion(f32[4,12,960]{2,1,0:T(8,128)S(1)} %get-tuple-element.513, s32[]{:T(128)S(6)} %copy.387, f32[12,960]{1,0:T(8,128)S(1)} %fusion.300, s32[16384]{0:T(1024)S(1)} %select_select_fusion.5, f32[4,12,16384]{2,1,0:T(8,128)} %get-tuple-element.519), kind=kOutput, calls=%fused_computation.25.clone.1 | convolution fusion | flops 393227520 | bytes 721920 | tf_op jit(solution)/shard_map/while/body/eval_jaxpr/dot_general | solution.py:73
  528.7 24.4 %all-reduce.22 = (bf16[768]{0:T(1024)(128)(2,1)S(1)}, bf16[768]{0:T(1024)(128)(2,1)S(1)}, bf16[768]{0:T(1024)(128)(2,1)S(1)}, bf16[768]{0:T(1024)(128)(2,1)S(1)}...) all-reduce(f32[768]{0:T(1024)S(1)} %add.823, ...), channel_id=2, replica_groups=mesh['fsdp'=8,'rep'=4] {'fsdp'}, use_global_device_ids=true, to_apply=%region_26.29.clone | all-reduce | flops 22272 | bytes 133632
  559.7 42.5 %reduce-scatter.12.cloned.1.call-done = f32[384,768]{1,0:T(8,128)} async-done(((f32[3072,768]{1,0:T(8,128)}), f32[384,768]{1,0:T(8,128)}) %reduce-scatter.12.cloned.1.call-update) | async-done | bytes 1179664 | tf_op jit(solution)/shard_map/reduce_scatter | solution.py:358
  604.5 19.2 %all-reduce.24 = (bf16[96]{0:T(256)(128)(2,1)S(1)}, bf16[96]{0:T(256)(128)(2,1)S(1)}, bf16[96]{0:T(256)(128)(2,1)S(1)}, bf16[96]{0:T(256)(128)(2,1)S(1)}, bf16[1...) all-reduce(bf16[96]{0:T(256)(128)(2,1)S(1)} %dynamic-slice.56, ...), channel_id=1, replica_groups=mesh['fsdp'=8,'rep'=4] {'rep'}, use_global_device_ids=true, to_apply=%region_27.30 | all-reduce | flops 2784 | bytes 11136 | tf_op jit(solution)/shard_map/psum | solution.py:363
  636.4 46.4 %all-reduce.28.cloned.1.call-done = (bf16[96,2304]{1,0:T(8,128)(2,1)}, bf16[96,768]{1,0:T(8,128)(2,1)}, bf16[96,3072]{1,0:T(8,128)(2,1)}, bf16[384,768]{1,0:T(8,128)(2,1)}) async-done(((bf16[96,2304]{1,0:T(8,128)(2,1)}, bf16[96,768]{1,0:T(8,128)(2,1)}, bf16[96,3072]{1,0:T(8,128)(2,1)}, bf16[384,768]{1,0:T(8,128)(2,1)}), (bf16[96,2304]{1,0:T(8,128)(2,1)}, bf16[96,768]{1,0:T(8,128)(2,1)}, ...) | async-done | bytes 1769488 | tf_op jit(solution)/shard_map/psum | solution.py:365
  (514 shorter events, 262.2 us)
Async XLA Ops:
  7.2 43.6 %copy-start.2 = (bf16[2,2,256,768]{3,2,1,0:T(8,128)(2,1)S(1)}, bf16[2,2,256,768]{3,2,1,0:T(8,128)(2,1)}, u32[]{:S(2)}) copy-start(bf16[2,2,256,768]{3,2,1,0:T(8,128)(2,1)} %param.27) | copy-start | bytes 4718596
  7.2 52.2 %copy-start.76 = (bf16[120,12]{0,1:T(8,128)(2,1)S(1)}, bf16[120,12]{0,1:T(8,128)(2,1)}, u32[]{:S(2)}) copy-start(bf16[120,12]{0,1:T(8,128)(2,1)} %param.34) | copy-start | bytes 8644
  7.2 121.4 %all-gather.7.cloned.1.call-start = ((), (), s32[]{:S(2)}) async-start(), calls=%async_computation.4 | async-start | bytes 3981312 | tf_op jit(solution)/shard_map/all_gather | solution.py:163
  7.9 211.3 %all-gather.9.cloned.1.call-start = ((), (), s32[]{:S(2)}) async-start(), calls=%async_computation.5 | async-start | bytes 1327104 | tf_op jit(solution)/shard_map/all_gather | solution.py:167
  8.7 216.7 %all-gather.11.cloned.1.call-start = ((), (), s32[]{:S(2)}) async-start(), calls=%async_computation.6 | async-start | bytes 5308416 | tf_op jit(solution)/shard_map/all_gather | solution.py:172
  9.4 255.1 %all-gather.13.cloned.1.call-start = ((), (), s32[]{:S(2)}) async-start(), calls=%async_computation.7 | async-start | bytes 5308416 | tf_op jit(solution)/shard_map/all_gather | solution.py:174
  10.0 543.9 %reduce-scatter.8.cloned.1.call-start = ((), (), s32[]{:S(2)}) async-start(), calls=%async_computation.9 | async-start | bytes 2654208 | tf_op jit(solution)/shard_map/reduce_scatter | solution.py:351
  48.4 78.0 %copy-start.60 = (f32[768]{0:T(1024)}, f32[768]{0:T(1024)S(1)}, u32[]{:S(2)}) copy-start(f32[768]{0:T(1024)S(1)} %convert_element_type.442) | copy-start | bytes 9220
  48.4 76.7 %copy-start.62 = (f32[768]{0:T(1024)}, f32[768]{0:T(1024)S(1)}, u32[]{:S(2)}) copy-start(f32[768]{0:T(1024)S(1)} %convert_element_type.460) | copy-start | bytes 9220
  50.7 75.7 %copy-start.64 = (f32[1,2,2,128]{3,1,2,0:T(2,128)}, f32[1,2,2,128]{3,1,2,0:T(2,128)S(1)}, u32[]{:S(2)}) copy-start(f32[1,2,2,128]{3,1,2,0:T(2,128)S(1)} %copy.283) | copy-start | bytes 6148
  50.7 75.6 %copy-start.66 = (f32[1,2,2,128]{3,1,2,0:T(2,128)}, f32[1,2,2,128]{3,1,2,0:T(2,128)S(1)}, u32[]{:S(2)}) copy-start(f32[1,2,2,128]{3,1,2,0:T(2,128)S(1)} %copy.286) | copy-start | bytes 6148
  51.4 75.0 %copy-start.68 = (f32[1,2,2,128]{3,1,2,0:T(2,128)}, f32[1,2,2,128]{3,1,2,0:T(2,128)S(1)}, u32[]{:S(2)}) copy-start(f32[1,2,2,128]{3,1,2,0:T(2,128)S(1)} %copy.284) | copy-start | bytes 6148
  51.4 75.0 %copy-start.70 = (f32[1,2,2,128]{3,1,2,0:T(2,128)}, f32[1,2,2,128]{3,1,2,0:T(2,128)S(1)}, u32[]{:S(2)}) copy-start(f32[1,2,2,128]{3,1,2,0:T(2,128)S(1)} %copy.287) | copy-start | bytes 6148
  128.6 56.0 %copy-start.72 = (s32[2,256]{1,0:T(2,128)}, s32[2,256]{1,0:T(2,128)S(1)}, u32[]{:S(2)}) copy-start(s32[2,256]{1,0:T(2,128)S(1)} %get-tuple-element.383) | copy-start | bytes 6148
  128.6 75.6 %copy-start.74 = (s32[2,256]{1,0:T(2,128)}, s32[2,256]{1,0:T(2,128)S(1)}, u32[]{:S(2)}) copy-start(s32[2,256]{1,0:T(2,128)S(1)} %get-tuple-element.384) | copy-start | bytes 6148
  225.4 8.1 %copy-start.24 = (f32[512,768]{1,0:T(8,128)S(1)}, f32[512,768]{1,0:T(8,128)}, u32[]{:S(2)}) copy-start(f32[512,768]{1,0:T(8,128)} %copy-done.23) | copy-start | bytes 4718596
  225.4 8.0 %copy-start.78 = (bf16[768,3072]{1,0:T(8,128)(2,1)S(1)}, bf16[768,3072]{1,0:T(8,128)(2,1)}, u32[]{:S(2)}) copy-start(bf16[768,3072]{1,0:T(8,128)(2,1)} %all-gather.11.cloned.1.call-done) | copy-start | bytes 14155780
  264.5 7.6 %copy-start.79 = (bf16[768,3072]{1,0:T(8,128)(2,1)S(1)}, bf16[768,3072]{1,0:T(8,128)(2,1)}, u32[]{:S(2)}) copy-start(bf16[768,3072]{1,0:T(8,128)(2,1)} %all-gather.11.cloned.1.call-done) | copy-start | bytes 14155780
  272.2 14.7 %slice-start.4 = ((s8[6291456]{0:T(1024)(128)(4,1)}), s8[4194304]{0:T(1024)(128)(4,1)S(1)}, s32[]{:S(2)}) async-start(s8[6291456]{0:T(1024)(128)(4,1)} %bitcast.401), calls=%async_computation.17 | async-start | bytes 8388608
  277.2 9.7 %slice-start.5 = ((s8[6291456]{0:T(1024)(128)(4,1)}), s8[2097152]{0:T(1024)(128)(4,1)S(1)}, s32[]{:S(2)}) async-start(s8[6291456]{0:T(1024)(128)(4,1)} %bitcast.401), calls=%async_computation.18 | async-start | bytes 4194304
  286.9 8.8 %copy-start.26 = (f32[512,768]{1,0:T(8,128)}, f32[512,768]{1,0:T(8,128)S(1)}, u32[]{:S(2)}) copy-start(f32[512,768]{1,0:T(8,128)S(1)} %get-tuple-element.370) | copy-start | bytes 4718596
  320.4 7.0 %copy-start.39 = (bf16[96,8,2,256]{3,1,2,0:T(8,128)(2,1)S(1)}, bf16[96,8,2,256]{3,1,2,0:T(8,128)(2,1)}, u32[]{:S(2)}) copy-start(bf16[96,8,2,256]{3,1,2,0:T(8,128)(2,1)} %copy-done.38) | copy-start | bytes 2359300
  320.4 7.0 %copy-start.48 = (bf16[512,768]{1,0:T(8,128)(2,1)S(1)}, bf16[512,768]{1,0:T(8,128)(2,1)}, u32[]{:S(2)}) copy-start(bf16[512,768]{1,0:T(8,128)(2,1)} %copy-done.47) | copy-start | bytes 2359300
  329.7 225.9 %reduce-scatter.6.cloned.1.call-start = ((), (), s32[]{:S(2)}) async-start(), calls=%async_computation.8 | async-start | bytes 7962624 | tf_op jit(solution)/shard_map/reduce_scatter | solution.py:347
  333.9 12.5 %slice-start.2 = ((s8[6291456]{0:T(1024)(128)(4,1)}), s8[4194304]{0:T(1024)(128)(4,1)S(1)}, s32[]{:S(2)}) async-start(s8[6291456]{0:T(1024)(128)(4,1)} %bitcast.350), calls=%async_computation.15 | async-start | bytes 8388608
  333.9 12.5 %slice-start.3 = ((s8[6291456]{0:T(1024)(128)(4,1)}), s8[2097152]{0:T(1024)(128)(4,1)S(1)}, s32[]{:S(2)}) async-start(s8[6291456]{0:T(1024)(128)(4,1)} %bitcast.350), calls=%async_computation.16 | async-start | bytes 4194304
  364.1 193.4 %reduce-scatter.10.cloned.1.call-start = ((), (), s32[]{:S(2)}) async-start(), calls=%async_computation.10 | async-start | bytes 10616832 | tf_op jit(solution)/shard_map/reduce_scatter | solution.py:356
  376.5 225.7 %reduce-scatter.12.cloned.1.call-start = ((), (), s32[]{:S(2)}) async-start(), calls=%async_computation.11 | async-start | bytes 10616832 | tf_op jit(solution)/shard_map/reduce_scatter | solution.py:358
  388.2 294.7 %all-reduce.28.cloned.1.call-start = ((), (), s32[]{:S(2)}) async-start(), calls=%async_computation.12 | async-start | bytes 3538944 | tf_op jit(solution)/shard_map/psum | solution.py:365
  559.7 73.0 %copy-start.8 = (f32[512,768]{1,0:T(8,128)S(1)}, f32[512,768]{1,0:T(8,128)}, u32[]{:S(2)}) copy-start(f32[512,768]{1,0:T(8,128)} %copy-done.7) | copy-start | bytes 4718596
  623.7 9.0 %copy-start.27 = (f32[512,768]{1,0:T(8,128)S(1)}, f32[512,768]{1,0:T(8,128)}, u32[]{:S(2)}) copy-start(f32[512,768]{1,0:T(8,128)} %copy-done.26) | copy-start | bytes 4718596
  623.7 9.0 %copy-start.52 = (f32[512,768]{1,0:T(8,128)S(1)}, f32[512,768]{1,0:T(8,128)}, u32[]{:S(2)}) copy-start(f32[512,768]{1,0:T(8,128)} %copy-done.51) | copy-start | bytes 4718596
  (70 other events, 255.3 us)
Sparse Core Ops, SparseCore 0:
  9.9 36.8 all-gather.6
  48.7 24.0 all-gather.8
  74.7 39.0 all-gather.10
  115.5 38.9 all-gather.12
  329.8 43.0 reduce-scatter.7
  376.6 65.4 reduce-scatter.5
  445.6 76.5 reduce-scatter.9
  525.7 76.4 reduce-scatter.11
  606.0 76.7 all-reduce.27
where the time goes:
time: 702 us; the launch traced here: 697 us
  matrix products  331 us (47%)
  local copies, waits for them, and re-layouts  94 us (13%)
  waiting for transfers between devices  91.7 us (13%)
  blocking collectives  86.4 us (12%)
  other arithmetic  72.2 us (10%)
  between operations  19.2 us (3%)
    unnamed x2, blocking collectives  50.2 us
    dot_general x4, matrix products, table_one_block(): jnp.dot(high_part, onehot, preferred_element_type=jnp.float32)  49.2 us
    dot_general x4, matrix products, table_one_block(): jnp.dot(low_part, onehot, preferred_element_type=jnp.float32)  49 us
    psum x1, waiting for transfers between devices, shards(): lax.psum(summed[2].astype(jnp.bfloat16), 'rep').astype(jnp.float32)  46.4 us
    reduce_scatter x1, waiting for transfers between devices, shards(): lax.psum_scatter(summed[12], 'fsdp', scatter_dimension=0, tiled=True)  42.5 us
    dot_general x4, matrix products, build_one_block(): return jnp.dot(table_cols, onehot, preferred_element_type=jnp.float32)  41.8 us
    dot_general x2, matrix products, shards(): jnp.dot(act_two, expand_full, preferred_element_type=jnp.float32)  36.4 us
    dot_general x8, matrix products, dot_rows(): lax.dot_general(left, right, (((0,), (0,)), ((), ())), preferred_element_...  33.7 us
  transfers between devices with their start and end apart: 9, of which 2 were waited for; matrix products, arithmetic and copies ran while one was open for 59% of the time, Pallas kernels for 0%

commit v1 on v0

v1 whole, which is shorter than its diff:
```python
import functools

import jax
import jax.numpy as jnp
from jax import lax
from jax.experimental import pallas as pl
from jax.experimental.pallas import tpu as pltpu
from jax.sharding import PartitionSpec as P

GH = 15
GW = 17
NREL = 960
SPAN = 2 * GW - 1
AHEAD = 2
CENTER = (GH - 1) * SPAN + GW - 1
HEAD = 64
SLOTS = 256

epsilon = 1e-06
negative = -1000000000.0
inv_root_tau = 0.3989422804014327
log2_e = 1.4426950408889634
VMEM_BYTES = 60 * 1024 * 1024
FAST_GROUP = 8

bf16 = jnp.bfloat16
f32 = jnp.float32


def dot_nn(left, right):
    return lax.dot_general(left, right, (((1,), (0,)), ((), ())), preferred_element_type=f32)


def dot_nt(left, right):
    return lax.dot_general(left, right, (((1,), (1,)), ((), ())), preferred_element_type=f32)


def normal_stats(values):
    center = values - jnp.mean(values, axis=-1, keepdims=True)
    inverse = lax.rsqrt(jnp.mean(center * center, axis=-1, keepdims=True) + epsilon)
    return center * inverse, inverse


def params(*semantics):
    return pltpu.CompilerParams(
        dimension_semantics=semantics, vmem_limit_bytes=VMEM_BYTES
    )


def cost(flops, nbytes):
    return pl.CostEstimate(flops=int(flops), bytes_accessed=int(nbytes), transcendentals=0)


def whole(shape):
    return pl.BlockSpec(shape, lambda *_: (0,) * len(shape))


any_spec = pl.BlockSpec(memory_space=pl.ANY)


def piece_copies(pieces, offsets, target, sems, base=0):
    return [
        pltpu.make_async_copy(
            piece,
            target.at[pl.ds(pl.multiple_of(offsets[base + k], 16), piece.shape[0])],
            sems.at[k],
        )
        for k, piece in enumerate(pieces)
    ]


VEC = dict(
    gain_one=0,
    shift_one=1,
    query_bias=2,
    value_bias=3,
    out_bias=4,
    scale_one=5,
    gain_two=6,
    shift_two=7,
    reduce_bias=8,
    scale_two=9,
)


def row(vec_ref, name):
    k = VEC[name]
    return vec_ref[k : k + 1, :]


def prepare_body(x_ref, g_ref, vec_ref, act_ref, act_t_ref, down_t_ref, sum_ref):
    step = pl.program_id(0)
    unit, _ = normal_stats(x_ref[...].astype(f32))
    act = unit * row(vec_ref, "gain_one") + row(vec_ref, "shift_one")
    act_ref[...] = act.astype(bf16)
    act_t_ref[...] = act.astype(bf16).T
    d_down = (row(vec_ref, "scale_two") * g_ref[...].astype(f32)).astype(bf16)
    down_t_ref[...] = d_down.T

    @pl.when(step == 0)
    def _():
        sum_ref[...] = jnp.zeros_like(sum_ref)

    sum_ref[...] += jnp.sum(d_down.astype(f32), axis=0, keepdims=True)


def prepare(x, g, vecs):
    tokens, width = x.shape
    block = pl.BlockSpec((SLOTS, width), lambda i: (i, 0))
    block_t = pl.BlockSpec((width, SLOTS), lambda i: (0, i))
    return pl.pallas_call(
        prepare_body,
        grid=(tokens // SLOTS,),
        in_specs=[block, block, whole(vecs.shape)],
        out_specs=[block, block_t, block_t, whole((1, width))],
        out_shape=[
            jax.ShapeDtypeStruct((tokens, width), bf16),
            jax.ShapeDtypeStruct((width, tokens), bf16),
            jax.ShapeDtypeStruct((width, tokens), bf16),
            jax.ShapeDtypeStruct((1, width), f32),
        ],
        compiler_params=params("arbitrary"),
        cost_estimate=cost(40 * tokens * width, 10 * tokens * width),
        name="prepare",
    )(x, g, vecs)


def spread(first, flip):
    spots = lax.broadcasted_iota(jnp.int32, (SLOTS, 2 * SLOTS), 0) - 1
    lanes = lax.broadcasted_iota(jnp.int32, (SLOTS, 2 * SLOTS), 1)
    target = spots + (SPAN - GW) * ((spots * 241) >> 12)
    target = jnp.where(spots >= 0, target, -1)
    if flip:
        target = jnp.where(spots >= 0, 2 * SLOTS - 1 - target, -1)
    return (lanes == target).astype(f32).astype(bf16)


def border(shape):
    q_zero = lax.broadcasted_iota(jnp.int32, shape, 0) == 0
    p_zero = lax.broadcasted_iota(jnp.int32, shape, 1) == 0
    return q_zero, p_zero


def tiles_body(flat_ref, tile_ref, place):
    @pl.when(pl.program_id(0) == 0)
    def _():
        place[...] = spread(0, False)

    flat = flat_ref[0]
    wide = jnp.broadcast_to(flat, (2 * SLOTS, 4 * SLOTS))
    shifted = pltpu.roll(wide, 4 * SLOTS - CENTER - AHEAD, 1, stride=1, stride_axis=0)
    toeplitz = shifted[:, : 2 * SLOTS].astype(bf16)
    rows_at = dot_nn(place[...], toeplitz).astype(bf16)
    inner = dot_nt(rows_at, place[...])
    q_zero, p_zero = border(inner.shape)
    last = NREL - 1 + AHEAD
    edge = jnp.where(
        p_zero,
        jnp.where(q_zero, flat[:, last : last + 1], flat[:, last - 2 : last - 1]),
        flat[:, last - 1 : last],
    )
    tile_ref[0] = jnp.where(q_zero | p_zero, edge, inner).astype(bf16)


def build_tiles(flat):
    heads = flat.shape[0]
    return pl.pallas_call(
        tiles_body,
        grid=(heads,),
        in_specs=[pl.BlockSpec((1, 1, 4 * SLOTS), lambda h: (h, 0, 0))],
        out_specs=pl.BlockSpec((1, SLOTS, SLOTS), lambda h: (h, 0, 0)),
        out_shape=jax.ShapeDtypeStruct((heads, SLOTS, SLOTS), bf16),
        scratch_shapes=[pltpu.VMEM((SLOTS, 2 * SLOTS), bf16)],
        compiler_params=params("arbitrary"),
        cost_estimate=cost(heads * 12 * SLOTS**3, heads * 4 * SLOTS**2),
        name="build_tiles",
    )(flat)


def table_body(tile_ref, flat_ref, place, flipped):
    @pl.when(pl.program_id(0) == 0)
    def _():
        place[...] = spread(0, False)
        flipped[...] = spread(0, True)

    tile = tile_ref[0]
    q_zero, p_zero = border(tile.shape)
    inner = jnp.where(q_zero | p_zero, 0.0, tile).astype(bf16)
    columns_at = dot_nn(inner, place[...]).astype(bf16)
    spread_all = lax.dot_general(
        flipped[...], columns_at, (((0,), (0,)), ((), ())), preferred_element_type=f32
    )
    wide = jnp.concatenate([spread_all, jnp.zeros_like(spread_all)], axis=1)
    shift = CENTER - (2 * SLOTS - 1) + 1
    shifted = pltpu.roll(wide, shift % (4 * SLOTS), 1, stride=1, stride_axis=0)
    flat = jnp.sum(shifted, axis=0, keepdims=True)
    lanes = lax.broadcasted_iota(jnp.int32, flat.shape, 1)
    both = jnp.sum(jnp.where(q_zero & p_zero, tile, 0.0))
    query_only = jnp.sum(jnp.where(p_zero & ~q_zero, tile, 0.0))
    key_only = jnp.sum(jnp.where(q_zero & ~p_zero, tile, 0.0))
    flat = jnp.where(lanes == NREL, both, flat)
    flat = jnp.where(lanes == NREL - 2, query_only, flat)
    flat = jnp.where(lanes == NREL - 1, key_only, flat)
    flat_ref[0] = flat


def table_grad(tiles):
    heads = tiles.shape[0]
    return pl.pallas_call(
        table_body,
        grid=(heads,),
        in_specs=[pl.BlockSpec((1, SLOTS, SLOTS), lambda h: (h, 0, 0))],
        out_specs=pl.BlockSpec((1, 1, 4 * SLOTS), lambda h: (h, 0, 0)),
        out_shape=jax.ShapeDtypeStruct((heads, 1, 4 * SLOTS), f32),
        scratch_shapes=[pltpu.VMEM((SLOTS, 2 * SLOTS), bf16)] * 2,
        compiler_params=params("arbitrary"),
        cost_estimate=cost(heads * 12 * SLOTS**3, heads * 4 * SLOTS**2),
        name="table_grad",
    )(tiles)


def place_pair(spot_row, spot_column):
    shape = (SLOTS, SLOTS)
    by_slot = lax.broadcasted_iota(jnp.int32, shape, 1) == spot_column
    by_spot = lax.broadcasted_iota(jnp.int32, shape, 0) == spot_row
    return by_slot.astype(f32).astype(bf16), by_spot.astype(f32).astype(bf16)


def in_pair(block, head):
    rest = jnp.zeros_like(block)
    return jnp.concatenate([block, rest] if head % 2 == 0 else [rest, block], axis=0)


def attend_body(
    n_pieces,
    offsets,
    act_ref,
    vec_ref,
    row_ref,
    column_ref,
    tile_ref,
    *rest,
):
    pieces = rest[:n_pieces]
    value_ref, q_t_ref, k_t_ref, exp_ref, inv_ref, heads_t_ref, heads_ref, weight, sems = rest[
        n_pieces:
    ]
    width = act_ref.shape[1]

    @pl.when(pl.program_id(0) == 0)
    def _():
        copies = piece_copies(pieces, offsets, weight, sems)
        for copy in copies:
            copy.start()
        for copy in copies:
            copy.wait()

    act = act_ref[...]
    query = (dot_nn(act, weight[:, :width]) + row(vec_ref, "query_bias")) * 0.125
    q_t = query.astype(bf16).T
    keys = dot_nn(act, weight[:, width : 2 * width]).astype(bf16)
    k_t_ref[...] = keys.T
    q_t_ref[...] = q_t
    values = dot_nn(act, weight[:, 2 * width :]) + row(vec_ref, "value_bias")
    values = values.astype(bf16)
    value_ref[...] = values
    v_t = values.T
    by_slot, by_spot = place_pair(row_ref[0], column_ref[0])
    mask = jnp.where(column_ref[0] >= 0, 0.0, negative)
    mask = jnp.broadcast_to(mask, (SLOTS, SLOTS))
    heads_count = width // HEAD
    ones = jnp.ones((16, SLOTS), bf16)
    for head in range(heads_count):
        low, high = head * HEAD, (head + 1) * HEAD
        pair = slice(head // 2 * 2 * HEAD, (head // 2 + 1) * 2 * HEAD)
        right = dot_nn(tile_ref[head], by_spot).astype(bf16)
        left_all = jnp.concatenate([by_slot, keys[:, pair]], axis=1)
        right_all = jnp.concatenate([right, in_pair(q_t[low:high], head)], axis=0)
        scores = dot_nn(left_all, right_all) + mask
        peak = jnp.max(scores, axis=0, keepdims=True)
        exponent = jnp.exp(scores - peak).astype(bf16)
        exp_ref[0, head] = exponent
        summed = dot_nn(jnp.concatenate([v_t[low:high], ones], axis=0), exponent)
        inverse = 1.0 / summed[HEAD : HEAD + 1]
        inv_ref[0, head : head + 1, :] = inverse
        heads_t_ref[low:high, :] = (summed[:HEAD] * inverse).astype(bf16)
    heads_ref[...] = heads_t_ref[...].T


def attend(offsets, act, vecs, spots, tiles, pieces):
    tokens, width = act.shape
    images = tokens // SLOTS
    heads = width // HEAD
    block = pl.BlockSpec((SLOTS, width), lambda i, _: (i, 0))
    block_t = pl.BlockSpec((width, SLOTS), lambda i, _: (0, i))
    return pl.pallas_call(
        functools.partial(attend_body, len(pieces)),
        grid_spec=pltpu.PrefetchScalarGridSpec(
            num_scalar_prefetch=1,
            grid=(images,),
            in_specs=[
                block,
                whole(vecs.shape),
                pl.BlockSpec((1, 1, SLOTS), lambda i, _: (i, 0, 0)),
                pl.BlockSpec((1, SLOTS, 1), lambda i, _: (i, 0, 0)),
                whole(tiles.shape),
            ]
            + [any_spec] * len(pieces),
            out_specs=[
                block,
                block_t,
                block_t,
                pl.BlockSpec((1, heads, SLOTS, SLOTS), lambda i, _: (i, 0, 0, 0)),
                pl.BlockSpec((1, heads, SLOTS), lambda i, _: (i, 0, 0)),
                block_t,
                block,
            ],
            scratch_shapes=[
                pltpu.VMEM((width, 3 * width), bf16),
                pltpu.SemaphoreType.DMA((len(pieces),)),
            ],
        ),
        out_shape=[
            jax.ShapeDtypeStruct((tokens, width), bf16),
            jax.ShapeDtypeStruct((width, tokens), bf16),
            jax.ShapeDtypeStruct((width, tokens), bf16),
            jax.ShapeDtypeStruct((images, heads, SLOTS, SLOTS), bf16),
            jax.ShapeDtypeStruct((images, heads, SLOTS), f32),
            jax.ShapeDtypeStruct((width, tokens), bf16),
            jax.ShapeDtypeStruct((tokens, width), bf16),
        ],
        compiler_params=params("arbitrary"),
        cost_estimate=cost(6 * tokens * width * width * 1.6, 14 * tokens * width),
        name="attend",
    )(offsets, act, vecs, spots[:, None, :], spots[:, :, None], tiles, *pieces)


def project_body(n_pieces, offsets, heads_ref, x_ref, vec_ref, *rest):
    pieces = rest[:n_pieces]
    attended_ref, middle_ref, act_ref, act_t_ref, weight, sems = rest[n_pieces:]

    @pl.when(pl.program_id(0) == 0)
    def _():
        copies = piece_copies(pieces, offsets, weight, sems)
        for copy in copies:
            copy.start()
        for copy in copies:
            copy.wait()

    attended = dot_nn(heads_ref[...], weight[...]) + row(vec_ref, "out_bias")
    attended_ref[...] = attended
    middle = x_ref[...].astype(f32) + row(vec_ref, "scale_one") * attended
    middle_ref[...] = middle
    unit, _ = normal_stats(middle)
    act = (unit * row(vec_ref, "gain_two") + row(vec_ref, "shift_two")).astype(bf16)
    act_ref[...] = act
    act_t_ref[...] = act.T


def project(offsets, heads, x, vecs, pieces):
    tokens, width = x.shape
    block = pl.BlockSpec((SLOTS, width), lambda i, _: (i, 0))
    block_t = pl.BlockSpec((width, SLOTS), lambda i, _: (0, i))
    return pl.pallas_call(
        functools.partial(project_body, len(pieces)),
        grid_spec=pltpu.PrefetchScalarGridSpec(
            num_scalar_prefetch=1,
            grid=(tokens // SLOTS,),
            in_specs=[block, block, whole(vecs.shape)] + [any_spec] * len(pieces),
            out_specs=[block, block, block, block_t],
            scratch_shapes=[
                pltpu.VMEM((width, width), bf16),
                pltpu.SemaphoreType.DMA((len(pieces),)),
            ],
        ),
        out_shape=[
            jax.ShapeDtypeStruct((tokens, width), f32),
            jax.ShapeDtypeStruct((tokens, width), f32),
            jax.ShapeDtypeStruct((tokens, width), bf16),
            jax.ShapeDtypeStruct((width, tokens), bf16),
        ],
        compiler_params=params("arbitrary"),
        cost_estimate=cost(2 * tokens * width * width, 16 * tokens * width),
        name="project",
    )(offsets, heads, x, vecs, *pieces)


def gelu_pair(hidden):
    bell = jnp.exp2(hidden * hidden * (-0.5 * log2_e))
    t = 1.0 / (1.0 + jnp.abs(hidden) * (0.3275911 * 0.7071067811865476))
    poly = 0.5 * 1.061405429
    poly = poly * t - 0.5 * 1.453152027
    poly = poly * t + 0.5 * 1.421413741
    poly = poly * t - 0.5 * 0.284496736
    poly = poly * t + 0.5 * 0.254829592
    tail = poly * t * bell
    phi = jnp.where(hidden >= 0.0, 1.0 - tail, tail)
    return hidden * phi, phi + hidden * bell * inv_root_tau


FF_BLOCK = 512


def expand_body(n_pieces, offsets, act_ref, bias_ref, *rest):
    pieces = rest[:n_pieces]
    active_ref, slope_ref, weight, sems = rest[n_pieces:]
    step = pl.program_id(0)

    @pl.when(step == 0)
    def _():
        copies = piece_copies(pieces, offsets, weight, sems)
        for copy in copies:
            copy.start()
        for copy in copies:
            copy.wait()

    start = pl.multiple_of(step * FF_BLOCK, FF_BLOCK)
    part = weight[:, pl.ds(start, FF_BLOCK)]
    for base in range(0, act_ref.shape[0], SLOTS):
        rows = slice(base, base + SLOTS)
        hidden = dot_nn(act_ref[rows, :], part) + bias_ref[...]
        active, slope = gelu_pair(hidden)
        active_ref[rows, :] = active.astype(bf16)
        slope_ref[rows, :] = slope.astype(bf16)


def expand(offsets, act, bias, pieces):
    tokens, width = act.shape
    hidden = bias.shape[1]
    block = pl.BlockSpec((tokens, FF_BLOCK), lambda i, _: (0, i))
    return pl.pallas_call(
        functools.partial(expand_body, len(pieces)),
        grid_spec=pltpu.PrefetchScalarGridSpec(
            num_scalar_prefetch=1,
            grid=(hidden // FF_BLOCK,),
            in_specs=[whole(act.shape), pl.BlockSpec((1, FF_BLOCK), lambda i, _: (0, i))]
            + [any_spec] * len(pieces),
            out_specs=[block, block],
            scratch_shapes=[
                pltpu.VMEM((width, hidden), bf16),
                pltpu.SemaphoreType.DMA((len(pieces),)),
            ],
        ),
        out_shape=[jax.ShapeDtypeStruct((tokens, hidden), bf16)] * 2,
        compiler_params=params("arbitrary"),
        cost_estimate=cost(2 * tokens * width * hidden * 1.5, 4 * tokens * hidden),
        name="expand",
    )(offsets, act, bias, *pieces)


def reduce_body(
    counts,
    offsets,
    active_ref,
    slope_ref,
    g_ref,
    middle_ref,
    attended_ref,
    vec_ref,
    *rest,
):
    n_reduce, n_expand, n_out = counts
    n_all = n_reduce + n_expand + n_out
    pieces = rest[:n_all]
    (
        out_ref,
        d_hidden_ref,
        d_middle_ref,
        d_att_ref,
        d_heads_t_ref,
        hidden_sum_ref,
        sum_ref,
        weight_r,
        weight_e,
        weight_o,
        sems,
    ) = rest[n_all:]
    step = pl.program_id(0)

    def copies_of(which):
        if which == 0:
            return piece_copies(pieces[:n_reduce], offsets, weight_r, sems.at[0], 0)
        if which == 1:
            mine = pieces[n_reduce : n_reduce + n_expand]
            return piece_copies(mine, offsets, weight_e, sems.at[1], n_reduce)
        return piece_copies(
            pieces[n_reduce + n_expand :], offsets, weight_o, sems.at[2], n_reduce + n_expand
        )

    @pl.when(step == 0)
    def _():
        for which in range(3):
            for copy in copies_of(which):
                copy.start()
        hidden_sum_ref[...] = jnp.zeros_like(hidden_sum_ref)
        sum_ref[...] = jnp.zeros_like(sum_ref)
        for copy in copies_of(0):
            copy.wait()

    g = g_ref[...].astype(f32)
    d_down = (row(vec_ref, "scale_two") * g).astype(bf16)
    d_active = dot_nt(d_down, weight_r[...])
    d_hidden = (d_active * slope_ref[...].astype(f32)).astype(bf16)
    d_hidden_ref[...] = d_hidden
    hidden_sum_ref[...] += jnp.sum(d_hidden.astype(f32), axis=0, keepdims=True)
    down = dot_nn(active_ref[...], weight_r[...]) + row(vec_ref, "reduce_bias")
    middle = middle_ref[...]
    out_ref[...] = (middle + row(vec_ref, "scale_two") * down).astype(bf16)

    @pl.when(step == 0)
    def _():
        for which in (1, 2):
            for copy in copies_of(which):
                copy.wait()

    d_act = dot_nt(d_hidden, weight_e[...])
    unit, inverse = normal_stats(middle)
    scaled = d_act * row(vec_ref, "gain_two")
    d_middle = g + inverse * (
        scaled
        - jnp.mean(scaled, axis=-1, keepdims=True)
        - unit * jnp.mean(scaled * unit, axis=-1, keepdims=True)
    )
    d_middle_ref[...] = d_middle
    d_att = (row(vec_ref, "scale_one") * d_middle).astype(bf16)
    d_att_ref[...] = d_att
    d_heads_t_ref[...] = dot_nt(weight_o[...], d_att).astype(bf16)

    def column(values):
        return jnp.sum(values, axis=0, keepdims=True)

    sum_ref[0:1] += column(g * down)
    sum_ref[1:2] += column(d_act * unit)
    sum_ref[2:3] += column(d_act)
    sum_ref[3:4] += column(d_middle * attended_ref[...])
    sum_ref[4:5] += column(d_att.astype(f32))


def reduce_back(offsets, active, slope, g, middle, attended, vecs, reduce_p, expand_p, out_p):
    tokens, hidden = active.shape
    width = g.shape[1]
    counts = (len(reduce_p), len(expand_p), len(out_p))
    block = pl.BlockSpec((SLOTS, width), lambda i, _: (i, 0))
    block_t = pl.BlockSpec((width, SLOTS), lambda i, _: (0, i))
    block_f = pl.BlockSpec((SLOTS, hidden), lambda i, _: (i, 0))
    return pl.pallas_call(
        functools.partial(reduce_body, counts),
        grid_spec=pltpu.PrefetchScalarGridSpec(
            num_scalar_prefetch=1,
            grid=(tokens // SLOTS,),
            in_specs=[block_f, block_f, block, block, block, whole(vecs.shape)]
            + [any_spec] * sum(counts),
            out_specs=[
                block,
                block_f,
                block,
                block,
                block_t,
                whole((1, hidden)),
                whole((8, width)),
            ],
            scratch_shapes=[
                pltpu.VMEM((hidden, width), bf16),
                pltpu.VMEM((width, hidden), bf16),
                pltpu.VMEM((width, width), bf16),
                pltpu.SemaphoreType.DMA((3, max(counts))),
            ],
        ),
        out_shape=[
            jax.ShapeDtypeStruct((tokens, width), bf16),
            jax.ShapeDtypeStruct((tokens, hidden), bf16),
            jax.ShapeDtypeStruct((tokens, width), f32),
            jax.ShapeDtypeStruct((tokens, width), bf16),
            jax.ShapeDtypeStruct((width, tokens), bf16),
            jax.ShapeDtypeStruct((1, hidden), f32),
            jax.ShapeDtypeStruct((8, width), f32),
        ],
        compiler_params=params("arbitrary"),
        cost_estimate=cost(
            6 * tokens * width * hidden + 2 * tokens * width * width, 7 * tokens * hidden
        ),
        name="reduce_back",
    )(offsets, active, slope, g, middle, attended, vecs, *reduce_p, *expand_p, *out_p)


def attend_back_body(
    first,
    count,
    d_heads_t_ref,
    value_ref,
    q_t_ref,
    k_t_ref,
    exp_ref,
    inv_ref,
    row_ref,
    column_ref,
    d_mixed_ref,
    tile_ref,
):
    @pl.when(pl.program_id(0) == 0)
    def _():
        tile_ref[...] = jnp.zeros_like(tile_ref)

    by_slot, by_spot = place_pair(row_ref[0], column_ref[0])
    for k in range(count):
        head = first + k
        low, high = k * HEAD, (k + 1) * HEAD
        pair = slice(k // 2 * 2 * HEAD, (k // 2 + 1) * 2 * HEAD)
        inverse = inv_ref[0, head : head + 1, :]
        exponent = exp_ref[0, k]
        wide = exponent.astype(f32)
        d_out = d_heads_t_ref[low:high, :]
        d_probs = dot_nn(value_ref[:, pair], in_pair(d_out, k))
        inner = jnp.sum(d_probs * wide, axis=0, keepdims=True) * inverse
        d_scores = ((d_probs - inner) * inverse * wide).astype(bf16)
        d_query = dot_nn(k_t_ref[low:high, :], d_scores)
        d_mixed_ref[low:high, :] = (d_query.astype(bf16) * 0.125).astype(bf16)
        base = count * HEAD
        d_keys = dot_nt(q_t_ref[low:high, :], d_scores)
        d_mixed_ref[base + low : base + high, :] = d_keys.astype(bf16)
        d_values = dot_nt((d_out.astype(f32) * inverse).astype(bf16), exponent)
        d_mixed_ref[2 * base + low : 2 * base + high, :] = d_values.astype(bf16)
        columns_at = dot_nn(d_scores, by_slot).astype(bf16)
        tile_ref[k] += dot_nn(by_spot, columns_at)


def attend_back(first, count, d_heads_t, value, q_t, k_t, exponent, inverse, spots):
    width, tokens = d_heads_t.shape
    images = tokens // SLOTS
    heads = inverse.shape[1]
    part = count * HEAD
    at = first // count
    block_t = pl.BlockSpec((part, SLOTS), lambda i: (at, i))
    return pl.pallas_call(
        functools.partial(attend_back_body, first, count),
        grid=(images,),
        in_specs=[
            block_t,
            pl.BlockSpec((SLOTS, part), lambda i: (i, at)),
            block_t,
            block_t,
            pl.BlockSpec((1, count, SLOTS, SLOTS), lambda i: (i, at, 0, 0)),
            pl.BlockSpec((1, heads, SLOTS), lambda i: (i, 0, 0)),
            pl.BlockSpec((1, 1, SLOTS), lambda i: (i, 0, 0)),
            pl.BlockSpec((1, SLOTS, 1), lambda i: (i, 0, 0)),
        ],
        out_specs=[
            pl.BlockSpec((3 * part, SLOTS), lambda i: (0, i)),
            whole((count, SLOTS, SLOTS)),
        ],
        out_shape=[
            jax.ShapeDtypeStruct((3 * part, tokens), bf16),
            jax.ShapeDtypeStruct((count, SLOTS, SLOTS), f32),
        ],
        compiler_params=params("arbitrary"),
        cost_estimate=cost(images * count * 14 * SLOTS**3, 12 * tokens * part),
        name="attend_back",
    )(d_heads_t, value, q_t, k_t, exponent, inverse, spots[:, None, :], spots[:, :, None])


def input_body(groups, offsets, x_ref, d_middle_ref, vec_ref, *rest):
    d_mixed_refs = rest[: len(groups)]
    rest = rest[len(groups) :]
    pieces = rest[:-5]
    grad_ref, sum_ref, bias_ref, weight, sems = rest[-5:]
    step = pl.program_id(0)
    width = x_ref.shape[1]

    @pl.when(step == 0)
    def _():
        copies = piece_copies(pieces, offsets, weight, sems)
        for copy in copies:
            copy.start()
        sum_ref[...] = jnp.zeros_like(sum_ref)
        bias_ref[...] = jnp.zeros_like(bias_ref)
        for copy in copies:
            copy.wait()

    total = None
    ones = jnp.ones((16, SLOTS), bf16)
    for (first, count), ref in zip(groups, d_mixed_refs, strict=True):
        part = count * HEAD
        for k in range(3):
            at = k * width + first * HEAD
            block = ref[k * part : (k + 1) * part, :]
            term = dot_nn(weight[:, at : at + part], block)
            total = term if total is None else total + term
            if k != 1:
                line = k // 2
                bias_ref[line : line + 1, first * HEAD : first * HEAD + part] += dot_nt(
                    ones, block
                )[:1]
    d_act = total.T
    unit, inverse = normal_stats(x_ref[...].astype(f32))
    sum_ref[0:1] += jnp.sum(d_act * unit, axis=0, keepdims=True)
    sum_ref[1:2] += jnp.sum(d_act, axis=0, keepdims=True)
    scaled = d_act * row(vec_ref, "gain_one")
    grad_ref[...] = (
        d_middle_ref[...]
        + inverse
        * (
            scaled
            - jnp.mean(scaled, axis=-1, keepdims=True)
            - unit * jnp.mean(scaled * unit, axis=-1, keepdims=True)
        )
    ).astype(bf16)


def input_back(offsets, x, d_middle, vecs, groups, d_mixed, pieces):
    tokens, width = x.shape
    block = pl.BlockSpec((SLOTS, width), lambda i, _: (i, 0))
    return pl.pallas_call(
        functools.partial(input_body, groups),
        grid_spec=pltpu.PrefetchScalarGridSpec(
            num_scalar_prefetch=1,
            grid=(tokens // SLOTS,),
            in_specs=[block, block, whole(vecs.shape)]
            + [pl.BlockSpec((m.shape[0], SLOTS), lambda i, _: (0, i)) for m in d_mixed]
            + [any_spec] * len(pieces),
            out_specs=[block, whole((8, width)), whole((8, width))],
            scratch_shapes=[
                pltpu.VMEM((width, 3 * width), bf16),
                pltpu.SemaphoreType.DMA((len(pieces),)),
            ],
        ),
        out_shape=[
            jax.ShapeDtypeStruct((tokens, width), bf16),
            jax.ShapeDtypeStruct((8, width), f32),
            jax.ShapeDtypeStruct((8, width), f32),
        ],
        compiler_params=params("arbitrary"),
        cost_estimate=cost(6 * tokens * width * width, 14 * tokens * width),
        name="input_back",
    )(offsets, x, d_middle, vecs, *d_mixed, *pieces)


def columns_body(order, left_ref, right_ref, out_ref):
    out_ref[0] = dot_nn(left_ref[...], right_ref[...]).astype(bf16)


def grad_columns(order, left_t, right, shards):
    width, tokens = left_t.shape
    part = right.shape[1] // shards
    blocks = order.shape[0]
    return pl.pallas_call(
        columns_body,
        grid_spec=pltpu.PrefetchScalarGridSpec(
            num_scalar_prefetch=1,
            grid=(blocks,),
            in_specs=[
                whole(left_t.shape),
                pl.BlockSpec((tokens, part), lambda i, order: (0, order[i])),
            ],
            out_specs=pl.BlockSpec((1, width, part), lambda i, _: (i, 0, 0)),
        ),
        out_shape=jax.ShapeDtypeStruct((blocks, width, part), bf16),
        compiler_params=params("arbitrary"),
        cost_estimate=cost(2 * tokens * width * part * blocks, 2 * tokens * part * blocks),
        name="grad_columns",
    )(order, left_t, right)


def rows_body(steps, transposed, column, order, *refs):
    n = len(steps)
    lefts, rights = refs[:n], refs[n : 2 * n]
    out_ref, gathered, sems = refs[2 * n :]
    step = pl.program_id(0)
    blocks = out_ref.shape[0]
    part = out_ref.shape[1]

    @pl.when(step == 0)
    def _():
        copies = [
            pltpu.make_async_copy(
                left.at[pl.ds(pl.multiple_of(order[b] * part, 16), part)],
                gathered.at[which, pl.ds(b * part, part)],
                sems.at[which, b],
            )
            for which, left in enumerate(lefts)
            for b in range(blocks)
        ]
        for copy in copies:
            copy.start()
        for copy in copies:
            copy.wait()

    start = 0
    for which in range(n):

        @pl.when((step >= start) & (step < start + steps[which]))
        def _():
            dot = dot_nt if transposed else dot_nn
            result = dot(gathered[which], rights[which][...]).astype(bf16)
            for b in range(blocks):
                out_ref[b] = result[b * part : (b + 1) * part]

        start += steps[which]


def grad_rows(order, lefts, rights, shards, column, transposed):
    width, tokens = lefts[0].shape
    part = width // shards
    blocks = order.shape[0]
    side = 0 if transposed else 1
    steps = [right.shape[side] // column for right in rights]
    in_specs = [any_spec] * len(lefts)
    start = 0
    for right, many in zip(rights, steps, strict=True):

        def index(i, _, start=start, many=many):
            at = jnp.clip(i - start, 0, many - 1)
            return (at, 0) if transposed else (0, at)

        in_specs.append(pl.BlockSpec((column, tokens) if transposed else (tokens, column), index))
        start += many
    return pl.pallas_call(
        functools.partial(rows_body, steps, transposed, column),
        grid_spec=pltpu.PrefetchScalarGridSpec(
            num_scalar_prefetch=1,
            grid=(start,),
            in_specs=in_specs,
            out_specs=pl.BlockSpec((blocks, part, column), lambda i, _: (0, 0, i)),
            scratch_shapes=[
                pltpu.VMEM((len(lefts), blocks * part, tokens), bf16),
                pltpu.SemaphoreType.DMA((len(lefts), blocks)),
            ],
        ),
        out_shape=jax.ShapeDtypeStruct((blocks, part, start * column), bf16),
        compiler_params=params("arbitrary"),
        cost_estimate=cost(
            2 * tokens * blocks * part * start * column, 2 * tokens * start * column
        ),
        name="grad_rows",
    )(order, *lefts, *rights)


def swap(values, bit):
    return lax.ppermute(values, "fsdp", [(k, k ^ bit) for k in range(FAST_GROUP)])


def gather_pieces(shard):
    rows = shard.shape[0]
    half = rows // 2
    me = lax.axis_index("fsdp")
    x_one = swap(shard, 2)
    y_one = swap(shard, 4)
    first = swap(x_one[:half], 4)
    second = swap(y_one[half:], 2)
    pieces = [shard, x_one, y_one, first, second]
    bits = [0, 2, 4, 6, 6]
    extra = [0, 0, 0, 0, half]
    offsets = [(me ^ bit) * rows + more for bit, more in zip(bits, extra)]
    offsets += [(me ^ bit ^ 1) * rows + more for bit, more in zip(bits, extra)]
    pieces = pieces + [swap(piece, 1) for piece in pieces]
    return pieces, jnp.stack(offsets).astype(jnp.int32)


def add_all(*terms):
    total = terms[0].astype(f32)
    for term in terms[1:]:
        total = total + term.astype(f32)
    return total.astype(bf16)


def scatter_sum(keep, send):
    half = keep.shape[1] // 2
    other = swap(send, 1)
    a, b = slice(0, half), slice(half, None)
    x_send = add_all(keep[1::2, a], other[1::2, a])
    y_send = add_all(keep[2:, b], other[2:, b])
    x_got = swap(x_send, 2)
    y_got = swap(y_send, 4)
    y_next = add_all(keep[2, a], other[2, a], x_got[1])
    x_next = add_all(keep[1, b], other[1, b], y_got[1])
    y_last = swap(y_next, 4)
    x_last = swap(x_next, 2)
    top = add_all(keep[0, a], other[0, a], x_got[0], y_last)
    bottom = add_all(keep[0, b], other[0, b], y_got[0], x_last)
    return jnp.concatenate([top, bottom], axis=0)


def sum_copies(values, count):
    distance = 1
    while distance < count:
        got = lax.ppermute(values, "rep", [(k, k ^ distance) for k in range(count)])
        values = add_all(values, got) if distance * 2 < count else values.astype(f32) + got.astype(f32)
        distance *= 2
    return values


def sum_small(values, count):
    for bit in (1, 2, 4):
        values = values + swap(values, bit)
    distance = 1
    while distance < count:
        values = values + lax.ppermute(values, "rep", [(k, k ^ distance) for k in range(count)])
        distance *= 2
    return values


def slot_spots(sizes):
    heights = sizes[:, 0:1]
    widths = sizes[:, 1:2]
    slots = jnp.arange(SLOTS)[None, :]
    offset = jnp.maximum(slots - 1, 0)
    spot = 1 + offset // widths * GW + offset % widths
    spot = jnp.where(slots == 0, 0, spot)
    return jnp.where(slots < 1 + heights * widths, spot, -1).astype(jnp.int32)


HEAD_GROUPS = ((0, 8), (8, 4))


def shards(
    rep_count,
    tokens_in,
    image_sizes,
    gain_one,
    shift_one,
    project_in,
    query_bias,
    value_bias,
    bias_table,
    project_out,
    out_bias,
    scale_one,
    gain_two,
    shift_two,
    expand_weight,
    expand_bias,
    reduce_weight,
    reduce_bias,
    scale_two,
    cotangent,
):
    batches, images, slots, width = tokens_in.shape
    tokens = batches * images * slots
    heads = bias_table.shape[1]
    share = gain_one.shape[0]
    group = width // share
    fast = group == FAST_GROUP
    me = lax.axis_index("fsdp")
    x = tokens_in.reshape(tokens, width)
    g = cotangent.reshape(tokens, width)
    spots = slot_spots(image_sizes.reshape(batches * images, 2))

    vectors = [gain_one, shift_one, query_bias, value_bias, out_bias, scale_one]
    vectors += [gain_two, shift_two, reduce_bias, scale_two]
    small = jnp.concatenate(vectors + [expand_bias, bias_table.reshape(-1)])
    length = small.shape[0]
    padded = -(-length // 128) * 128
    small = jnp.pad(small, (0, padded - length)).reshape(padded // 128, 128)
    small = lax.all_gather(small, "fsdp", axis=0, tiled=False).reshape(group, padded)
    count = len(vectors)
    vecs = small[:, : count * share].reshape(group, count, share)
    vecs = jnp.transpose(vecs, (1, 0, 2)).reshape(count, width).astype(f32)
    vecs = jnp.pad(vecs, ((0, 16 - count), (0, 0)))
    expand_row = small[:, count * share : count * share + expand_bias.shape[0]]
    expand_row = expand_row.reshape(1, -1).astype(f32)
    table = small[:, length - bias_table.size : length].reshape(NREL, heads)
    flat = jnp.pad(table.astype(f32).T, ((0, 0), (AHEAD, 4 * SLOTS - NREL - AHEAD)))[:, None, :]

    if fast:
        in_pieces, in_at = gather_pieces(project_in)
        out_pieces, out_at = gather_pieces(project_out)
        expand_pieces, expand_at = gather_pieces(expand_weight)
        reduce_pieces, reduce_at = gather_pieces(reduce_weight)
    else:
        zero = jnp.zeros((1,), jnp.int32)
        in_pieces, in_at = [lax.all_gather(project_in, "fsdp", axis=0, tiled=True)], zero
        out_pieces, out_at = [lax.all_gather(project_out, "fsdp", axis=0, tiled=True)], zero
        expand_pieces, expand_at = [lax.all_gather(expand_weight, "fsdp", axis=0, tiled=True)], zero
        reduce_pieces, reduce_at = [lax.all_gather(reduce_weight, "fsdp", axis=0, tiled=True)], zero

    act_one, act_one_t, d_down_t, grad_reduce_add = prepare(x, g, vecs)
    tiles = build_tiles(flat)
    value, q_t, k_t, exponent, inverse, heads_t, heads_out = attend(
        in_at, act_one, vecs, spots, tiles, in_pieces
    )
    attended, middle, act_two, act_two_t = project(out_at, heads_out, x, vecs, out_pieces)
    active, slope = expand(expand_at, act_two, expand_row, expand_pieces)

    keep_order = jnp.stack([me ^ bit for bit in (0, 2, 4, 6)]).astype(jnp.int32)
    send_order = keep_order ^ 1

    if fast:
        reduce_send = grad_columns(send_order, d_down_t, active, group)
        reduce_keep = grad_columns(keep_order, d_down_t, active, group)
        reduce_own = scatter_sum(reduce_keep, reduce_send)

    all_at = jnp.concatenate([reduce_at, expand_at, out_at])
    block_out, d_hidden, d_middle, d_att, d_heads_t, expand_sum, sums_two = reduce_back(
        all_at, active, slope, g, middle, attended, vecs, reduce_pieces, expand_pieces, out_pieces
    )

    if fast:
        lefts, rights = [act_two_t, heads_t], [d_hidden, d_att]
        middle_send = grad_rows(send_order, lefts, rights, group, 768, False)
        middle_keep = grad_rows(keep_order, lefts, rights, group, 768, False)
        middle_own = scatter_sum(middle_keep, middle_send)

    d_mixed, tile_grads, in_own = [], [], []
    for first, many in HEAD_GROUPS:
        part, tile_part = attend_back(
            first, many, d_heads_t, value, q_t, k_t, exponent, inverse, spots
        )
        d_mixed.append(part)
        tile_grads.append(tile_part)
        if fast:
            column = part.shape[0] // 3
            send = grad_rows(send_order, [act_one_t], [part], group, column, True)
            keep = grad_rows(keep_order, [act_one_t], [part], group, column, True)
            in_own.append(scatter_sum(keep, send))

    input_grad, sums_one, sums_mixed = input_back(
        in_at, x, d_middle, vecs, HEAD_GROUPS, d_mixed, in_pieces
    )
    table_flat = table_grad(jnp.concatenate(tile_grads))[:, 0, 1 : NREL + 1].T

    vector_grads = jnp.concatenate(
        [
            sums_one[0:2],
            sums_mixed[0:2],
            sums_two[4:5],
            sums_two[3:4],
            sums_two[1:3],
            grad_reduce_add,
            sums_two[0:1],
        ]
    )
    vector_grads = jnp.transpose(vector_grads.reshape(count, group, share), (1, 0, 2))
    small_grads = jnp.concatenate(
        [
            vector_grads.reshape(group, count * share),
            expand_sum.reshape(group, -1),
            table_flat.reshape(group, -1),
        ],
        axis=1,
    )

    if fast:
        small_grads = sum_small(small_grads, rep_count)
        own = lax.dynamic_slice_in_dim(small_grads, me, 1, axis=0)[0]
        grad_reduce = sum_copies(reduce_own, rep_count).T
        middle_all = sum_copies(middle_own, rep_count)
        grad_expand = middle_all[:, : expand_weight.shape[1]]
        grad_out = middle_all[:, expand_weight.shape[1] :]
        in_all = [sum_copies(value, rep_count) for value in in_own]
        parts = []
        for k in range(3):
            for (first, many), value in zip(HEAD_GROUPS, in_all):
                parts.append(value[:, k * many * HEAD : (k + 1) * many * HEAD])
        grad_in = jnp.concatenate(parts, axis=1)
    else:

        def total(values):
            values = lax.psum_scatter(values, "fsdp", scatter_dimension=0, tiled=True)
            return lax.psum(values.astype(bf16), "rep").astype(f32)

        parts = []
        for k in range(3):
            for (first, many), value in zip(HEAD_GROUPS, d_mixed):
                parts.append(value[k * many * HEAD : (k + 1) * many * HEAD])
        own = lax.psum_scatter(small_grads, "fsdp", scatter_dimension=0, tiled=True)
        own = lax.psum(own, "rep")[0]
        grad_in = total(dot_nt(act_one_t, jnp.concatenate(parts, axis=0)))
        grad_out = total(dot_nn(heads_t, d_att))
        grad_expand = total(dot_nn(act_two_t, d_hidden))
        grad_reduce = total(dot_nn(d_down_t, active).T)

    own_vectors = [own[k * share : (k + 1) * share] for k in range(count)]
    own_expand = own[count * share : count * share + expand_bias.shape[0]]
    own_table = own[count * share + expand_bias.shape[0] :].reshape(bias_table.shape)
    shape = tokens_in.shape
    return (
        block_out.reshape(shape),
        input_grad.reshape(shape),
        own_vectors[0],
        own_vectors[1],
        grad_in,
        own_vectors[2],
        own_vectors[3],
        own_table,
        grad_out,
        own_vectors[4],
        own_vectors[5],
        own_vectors[6],
        own_vectors[7],
        grad_expand,
        own_expand,
        grad_reduce,
        own_vectors[8],
        own_vectors[9],
    )


def solution(mesh):
    by_image = P(None, ("fsdp", "rep"), None, None)
    line = P("fsdp")
    matrix = P("fsdp", None)
    return jax.shard_map(
        functools.partial(shards, mesh.shape["rep"]),
        mesh=mesh,
        in_specs=(
            by_image,
            P(None, ("fsdp", "rep"), None),
            line,
            line,
            matrix,
            line,
            line,
            matrix,
            matrix,
            line,
            line,
            line,
            line,
            matrix,
            line,
            matrix,
            line,
            line,
            by_image,
        ),
        out_specs=(
            by_image,
            by_image,
            line,
            line,
            matrix,
            line,
            line,
            matrix,
            matrix,
            line,
            line,
            line,
            line,
            matrix,
            line,
            matrix,
            line,
            line,
        ),
        check_vma=False,
    )
```

time: 702 us -> 486 us (0.69)
  matrix products: 331 us -> 0 us
  Pallas kernels: 0 us -> 222 us
  blocking collectives: 86.4 us -> 9.13 us
  local copies, waits for them, and re-layouts: 94 us -> 25.9 us
  starting transfers between devices: 0.97 us -> 48.6 us
  waiting for transfers between devices: 91.7 us -> 138 us
  other arithmetic: 72.2 us -> 33.2 us
  between operations: 19.2 us -> 2.1 us
    dot_general x52 -> x0, matrix products: 331 us -> none  [the longest x4 49.2 us: table_one_block(): jnp.dot(high_part, onehot, preferred_element_type=jnp.float32)]
    pallas_call x0 -> x18, Pallas kernels: none -> 222 us  [the longest x6 44.2 us: grad_rows(): pl.pallas_call(functools.partial(rows_body, steps, transposed, column), g...]
    ppermute x0 -> x69, waiting for transfers between devices: none -> 138 us  [the longest x8 74.7 us: sum_copies(): got = lax.ppermute(values, 'rep', [(k, k ^ distance) for k in range(count)])]
    unnamed x2 -> x0, blocking collectives: 50.2 us -> none
    ppermute x0 -> x69, starting transfers between devices: none -> 48.6 us  [the longest x59 41.6 us: swap(): lax.ppermute(values, 'fsdp', [(k, k ^ bit) for k in range(FAST_GROUP)])]
    psum x1 -> x0, waiting for transfers between devices: 46.4 us -> none  [shards(): lax.psum(summed[2].astype(jnp.bfloat16), 'rep').astype(jnp.float32)]
    reduce_scatter x4 -> x0, waiting for transfers between devices: 42.5 us -> none  [the longest x1 42.5 us: shards(): lax.psum_scatter(summed[12], 'fsdp', scatter_dimension=0, tiled=True)]
    unnamed x236 -> x84, local copies, waits for them, and re-layouts: 33.5 us -> 5.92 us
  transfers between devices with their start and end apart: 9 -> 69, of which waited for: 2 -> 26; matrix products, arithmetic and copies ran while one was open for 59% -> 10% of each run, Pallas kernels for 0% -> 29%
where the time goes in v1:
time: 486 us; the launch traced here: 480 us
  Pallas kernels  222 us (46%)
  waiting for transfers between devices  138 us (28%)
  starting transfers between devices  48.6 us (10%)
  other arithmetic  33.2 us (7%)
  local copies, waits for them, and re-layouts  25.9 us (5%)
  blocking collectives  9.13 us (2%)
    ppermute x8, waiting for transfers between devices, sum_copies(): got = lax.ppermute(values, 'rep', [(k, k ^ distance) for k in range(count)])  74.7 us
    ppermute x59, waiting for transfers between devices, swap(): lax.ppermute(values, 'fsdp', [(k, k ^ bit) for k in range(FAST_GROUP)])  63.6 us
    pallas_call x6, Pallas kernels, grad_rows(): pl.pallas_call(functools.partial(rows_body, steps, transposed, column), g...  44.2 us
    ppermute x59, starting transfers between devices, swap(): lax.ppermute(values, 'fsdp', [(k, k ^ bit) for k in range(FAST_GROUP)])  41.6 us
    pallas_call x1, Pallas kernels, attend(): pl.pallas_call(functools.partial(attend_body, len(pieces)), grid_spec=plt...  34.9 us
    pallas_call x1, Pallas kernels, reduce_back(): pl.pallas_call(functools.partial(reduce_body, counts), grid_spec=pltpu.Pr...  31.2 us
    pallas_call x2, Pallas kernels, attend_back(): pl.pallas_call(functools.partial(attend_back_body, first, count), grid=(i...  28.7 us
    pallas_call x1, Pallas kernels, expand(): pl.pallas_call(functools.partial(expand_body, len(pieces)), grid_spec=plt...  20.3 us
  transfers between devices with their start and end apart: 69, of which 26 were waited for; matrix products, arithmetic and copies ran while one was open for 10% of the time, Pallas kernels for 29%

profile of v1, /device:TPU:0, one launch (start us, length us, event | category | flops | bytes accessed | tf_op | source)
XLA Modules:
  0.0 479.6 jit_solution(2424895885479315568)
XLA Ops:
  6.6 7.5 %concatenate.32 = bf16[2784]{0:T(1024)(128)(2,1)S(1)} concatenate(bf16[96]{0:T(256)(128)(2,1)} %param.21, bf16[96]{0:T(256)(128)(2,1)} %param.22, bf16[96]{0:T(256)(128)(2,1)} %param.24, bf16[96]{0:T(256)(128)(2,1)} %param.25, bf16[96]{0:T(256)(128)(2,1)} %param.28, bf16[96]{0:T(256)(128)(2,1)} %param.29, bf16[96]{0:T(256)(128)(2,1)} %param.30, bf16[96]{0:T(256)(128)(2,1)} %param.31, ...), dimensions={0} | concatenate | bytes 11136 | tf_op jit(solution)/shard_map/concatenate | solution.py:949
  14.1 9.1 %all_gather.3 = bf16[8,22,128]{2,1,0:T(8,128)(2,1)S(1)} all-gather(bf16[1,22,128]{2,1,0:T(8,128)(2,1)S(1)} %pad_bitcast_fusion), channel_id=1, replica_groups=mesh['fsdp'=8,'rep'=4] {'fsdp'}, dimensions={0}, use_global_device_ids=true | all-gather | bytes 50688 | tf_op jit(solution)/shard_map/all_gather | solution.py:953
  35.7 9.1 %build_tiles.1.tile_ref = bf16[12,256,256]{2,1,0:T(8,128)(2,1)} custom-call(f32[12,1,1024]{2,1,0:T(1,128)} %reshape.877.flat_ref), custom_call_target="tpu_custom_call" | custom-call | flops 2415919104 | bytes 3145728 | tf_op jit(solution)/shard_map/build_tiles/pallas_call | solution.py:167
  49.8 5.5 %collective-permute-done.19.rest_2_.rest_12_ = bf16[96,3072]{1,0:T(8,128)(2,1)S(1)} collective-permute-done((bf16[96,3072]{1,0:T(8,128)(2,1)}, bf16[96,3072]{1,0:T(8,128)(2,1)S(1)}, u32[]{:S(2)}, u32[]{:S(2)}) %collective-permute-start.19) | collective-permute-done | bytes 589856 | tf_op jit(solution)/shard_map/ppermute | solution.py:838
  56.7 15.5 %collective-permute-done.2.rest_3_.rest_5_ = bf16[48,2304]{1,0:T(8,128)(2,1)S(1)} collective-permute-done((bf16[48,2304]{1,0:T(8,128)(2,1)S(1)}, bf16[48,2304]{1,0:T(8,128)(2,1)S(1)}, u32[]{:S(2)}, u32[]{:S(2)}) %collective-permute-start.2) | collective-permute-done | bytes 221216 | tf_op jit(solution)/shard_map/ppermute | solution.py:838
  81.7 6.0 %prepare.1 = (bf16[1024,768]{1,0:T(8,128)(2,1)}, bf16[768,1024]{1,0:T(8,128)(2,1)}, bf16[768,1024]{1,0:T(8,128)(2,1)}, f32[1,768]{1,0:T(1,128)}) custom-call(bf16[1024,768]{1,0:T(8,128)(2,1)} %bitcast.130, bf16[1024,768]{1,0:T(8,128)(2,1)} %bitcast.128, f32[16,768]{1,0:T(8,128)} %pad_convert_fusion.1.vec_ref), custom_call_target="tpu_custom_call" | custom-call | flops 31457280 | bytes 7864320 | tf_op jit(solution)/shard_map/prepare/pallas_call | solution.py:111
  87.7 11.0 %fusion.8.column_ref = s32[4,256,1]{2,1,0:T(8,128)} fusion(s32[4]{0:T(128)S(1)} %copy-done.16, s32[4]{0:T(128)S(1)} %bitcast.143, s32[256]{0:T(256)S(1)} %get-tuple-element.196, s32[4]{0:T(128)S(1)} %copy-done.20, s32[4]{0:T(128)S(1)} %copy-done.18, s32[256]{0:T(256)S(1)} %get-tuple-element.197, pred[4]{0:T(512)(128)(4,1)S(1)} %compare_bitcast_fusion, ...), kind=kLoop, calls=%fused_computation.36 | loop fusion | flops 20480 | bytes 6468 | tf_op jit(solution)/shard_map/jit(_where)/select_n | solution.py:908
  100.3 34.9 %attend.1 = (bf16[1024,768]{1,0:T(8,128)(2,1)}, bf16[768,1024]{1,0:T(8,128)(2,1)}, bf16[768,1024]{1,0:T(8,128)(2,1)}, bf16[4,12,256,256]{3,2,1,0:T(8,128)(2,1)},...) custom-call(s32[10]{0:T(128)} %stack.120.offsets, ...), custom_call_target="tpu_custom_call" | custom-call | flops 5798205952 | bytes 11010048 | tf_op jit(solution)/shard_map/attend/pallas_call | solution.py:296
  135.3 8.7 %project.1 = (f32[1024,768]{1,0:T(8,128)}, f32[1024,768]{1,0:T(8,128)}, bf16[1024,768]{1,0:T(8,128)(2,1)}, bf16[768,1024]{1,0:T(8,128)(2,1)}) custom-call(s32[10]{0:T(128)} %stack.120.offsets, bf16[1024,768]{1,0:T(8,128)(2,1)} %get-tuple-element.50.heads_ref, bf16[1024,768]{1,0:T(8,128)(2,1)} %bitcast.131, f32[16,768]{1,0:T(8,128)} %pad_convert_fusion.1.vec_ref, ...), custom_call_target="tpu_custom_call" | custom-call | flops 1207959552 | bytes 12582912 | tf_op jit(solution)/shard_map/project/pallas_call | solution.py:364
  145.9 20.3 %expand.1 = (bf16[1024,3072]{1,0:T(8,128)(2,1)}, bf16[1024,3072]{1,0:T(8,128)(2,1)}) custom-call(s32[10]{0:T(128)} %stack.120.offsets, bf16[1024,768]{1,0:T(8,128)(2,1)} %get-tuple-element.51.act_ref, f32[1,3072]{1,0:T(1,128)} %bitcast.140, bf16[96,3072]{1,0:T(8,128)(2,1)} %rest_10_.1, bf16[96,3072]{1,0:T(8,128)(2,1)} %copy-done.6, ...), custom_call_target="tpu_custom_call" | custom-call | flops 7247757312 | bytes 12582912 | tf_op jit(solution)/shard_map/expand/pallas_call | solution.py:431
  167.2 31.2 %reduce_back.1 = (bf16[1024,768]{1,0:T(8,128)(2,1)}, bf16[1024,3072]{1,0:T(8,128)(2,1)}, f32[1024,768]{1,0:T(8,128)}, bf16[1024,768]{1,0:T(8,128)(2,1)}, bf16[76...) custom-call(s32[30]{0:T(128)} %concatenate.31.offsets, ...), custom_call_target="tpu_custom_call" | custom-call | flops 15703474176 | bytes 22020096 | tf_op jit(solution)/shard_map/reduce_back/pallas_call | solution.py:546
  198.4 10.7 %attend_back.3 = (bf16[768,1024]{1,0:T(8,128)(2,1)}, f32[4,256,256]{2,1,0:T(8,128)}) custom-call(bf16[768,1024]{1,0:T(8,128)(2,1)} %get-tuple-element.58.d_heads_t_ref, bf16[1024,768]{1,0:T(8,128)(2,1)} %get-tuple-element.59.value_ref, bf16[768,1024]{1,0:T(8,128)(2,1)} %get-tuple-element.60.q_t_ref, bf16[768,1024]{1,0:T(8,128)(2,1)} %get-tuple-element.61.k_t_ref, ...), custom_call_target="tpu_custom_call" | custom-call | flops 3758096384 | bytes 3145728 | tf_op jit(solution)/shard_map/attend_back/pallas_call | solution.py:634
  209.2 18.0 %attend_back.2 = (bf16[1536,1024]{1,0:T(8,128)(2,1)}, f32[8,256,256]{2,1,0:T(8,128)}) custom-call(bf16[768,1024]{1,0:T(8,128)(2,1)} %get-tuple-element.58.d_heads_t_ref, bf16[1024,768]{1,0:T(8,128)(2,1)} %get-tuple-element.59.value_ref, bf16[768,1024]{1,0:T(8,128)(2,1)} %get-tuple-element.60.q_t_ref, bf16[768,1024]{1,0:T(8,128)(2,1)} %get-tuple-element.61.k_t_ref, ...), custom_call_target="tpu_custom_call" | custom-call | flops 7516192768 | bytes 6291456 | tf_op jit(solution)/shard_map/attend_back/pallas_call | solution.py:634
  227.2 3.5 pad_maximum_fusion.tile_ref
  230.7 11.7 %table_grad.1 = f32[12,1,1024]{2,1,0:T(1,128)} custom-call(f32[12,256,256]{2,1,0:T(8,128)} %pad_maximum_fusion.tile_ref), custom_call_target="tpu_custom_call" | custom-call | flops 2415919104 | bytes 3145728 | tf_op jit(solution)/shard_map/table_grad/pallas_call | solution.py:209
  243.8 12.3 %input_back.1 = (bf16[1024,768]{1,0:T(8,128)(2,1)}, f32[8,768]{1,0:T(8,128)}, f32[8,768]{1,0:T(8,128)}) custom-call(s32[10]{0:T(128)} %stack.120.offsets, bf16[1024,768]{1,0:T(8,128)(2,1)} %bitcast.132, f32[1024,768]{1,0:T(8,128)} %get-tuple-element.57.d_middle_ref, f32[16,768]{1,0:T(8,128)} %pad_convert_fusion.1.vec_ref, ...), custom_call_target="tpu_custom_call" | custom-call | flops 3623878656 | bytes 11010048 | tf_op jit(solution)/shard_map/input_back/pallas_call | solution.py:712
  259.4 10.0 %grad_rows.10 = bf16[4,96,3840]{2,1,0:T(8,128)(2,1)} custom-call(s32[4]{0:T(128)} %get-tuple-element.153.order, bf16[768,1024]{1,0:T(8,128)(2,1)} %get-tuple-element.75.refs_0_, bf16[768,1024]{1,0:T(8,128)(2,1)} %get-tuple-element.76.refs_1_, bf16[1024,3072]{1,0:T(8,128)(2,1)} %get-tuple-element.77.refs_2_, bf16[1024,768]{1,0:T(8,128)(2,1)} %get-tuple-element.78.refs_3_), custom_call_target="tpu_custom_call" | custom-call | flops 3019898880 | bytes 7864320 | tf_op jit(solution)/shard_map/grad_rows/pallas_call | solution.py:816
  269.3 10.0 %grad_rows.11 = bf16[4,96,3840]{2,1,0:T(8,128)(2,1)} custom-call(s32[4]{0:T(128)} %get-tuple-element.152.order, bf16[768,1024]{1,0:T(8,128)(2,1)} %get-tuple-element.75.refs_0_, bf16[768,1024]{1,0:T(8,128)(2,1)} %get-tuple-element.76.refs_1_, bf16[1024,3072]{1,0:T(8,128)(2,1)} %get-tuple-element.77.refs_2_, bf16[1024,768]{1,0:T(8,128)(2,1)} %get-tuple-element.78.refs_3_), custom_call_target="tpu_custom_call" | custom-call | flops 3019898880 | bytes 7864320 | tf_op jit(solution)/shard_map/grad_rows/pallas_call | solution.py:816
  280.9 7.5 %grad_columns.3 = bf16[4,768,384]{2,1,0:T(8,128)(2,1)} custom-call(s32[4]{0:T(128)} %get-tuple-element.152.order, bf16[768,1024]{1,0:T(8,128)(2,1)} %get-tuple-element.79.left_ref, bf16[1024,3072]{1,0:T(8,128)(2,1)} %get-tuple-element.52.active_ref.right_ref), custom_call_target="tpu_custom_call" | custom-call | flops 2415919104 | bytes 3145728 | tf_op jit(solution)/shard_map/grad_columns/pallas_call | solution.py:745
  289.1 7.6 %grad_columns.2 = bf16[4,768,384]{2,1,0:T(8,128)(2,1)} custom-call(s32[4]{0:T(128)} %get-tuple-element.153.order, bf16[768,1024]{1,0:T(8,128)(2,1)} %get-tuple-element.79.left_ref, bf16[1024,3072]{1,0:T(8,128)(2,1)} %get-tuple-element.52.active_ref.right_ref), custom_call_target="tpu_custom_call" | custom-call | flops 2415919104 | bytes 3145728 | tf_op jit(solution)/shard_map/grad_columns/pallas_call | solution.py:745
  296.6 5.5 %grad_rows.9 = bf16[4,96,768]{2,1,0:T(8,128)(2,1)} custom-call(s32[4]{0:T(128)} %get-tuple-element.152.order, bf16[768,1024]{1,0:T(8,128)(2,1)} %get-tuple-element.74.refs_0_, bf16[768,1024]{1,0:T(8,128)(2,1)} %get-tuple-element.65.rest_1_.refs_1_), custom_call_target="tpu_custom_call" | custom-call | flops 603979776 | bytes 1572864 | tf_op jit(solution)/shard_map/grad_rows/pallas_call | solution.py:816
  303.9 6.5 %grad_rows.7 = bf16[4,96,1536]{2,1,0:T(8,128)(2,1)} custom-call(s32[4]{0:T(128)} %get-tuple-element.152.order, bf16[768,1024]{1,0:T(8,128)(2,1)} %get-tuple-element.74.refs_0_, bf16[1536,1024]{1,0:T(8,128)(2,1)} %get-tuple-element.64.rest_0_.refs_1_), custom_call_target="tpu_custom_call" | custom-call | flops 1207959552 | bytes 3145728 | tf_op jit(solution)/shard_map/grad_rows/pallas_call | solution.py:816
  313.1 6.5 %grad_rows.6 = bf16[4,96,1536]{2,1,0:T(8,128)(2,1)} custom-call(s32[4]{0:T(128)} %get-tuple-element.153.order, bf16[768,1024]{1,0:T(8,128)(2,1)} %get-tuple-element.74.refs_0_, bf16[1536,1024]{1,0:T(8,128)(2,1)} %get-tuple-element.64.rest_0_.refs_1_), custom_call_target="tpu_custom_call" | custom-call | flops 1207959552 | bytes 3145728 | tf_op jit(solution)/shard_map/grad_rows/pallas_call | solution.py:816
  320.2 5.8 %grad_rows.8 = bf16[4,96,768]{2,1,0:T(8,128)(2,1)} custom-call(s32[4]{0:T(128)} %get-tuple-element.153.order, bf16[768,1024]{1,0:T(8,128)(2,1)} %get-tuple-element.74.refs_0_, bf16[768,1024]{1,0:T(8,128)(2,1)} %get-tuple-element.65.rest_1_.refs_1_), custom_call_target="tpu_custom_call" | custom-call | flops 603979776 | bytes 1572864 | tf_op jit(solution)/shard_map/grad_rows/pallas_call | solution.py:816
  342.9 3.5 collective-permute-done.42
  369.1 4.5 collective-permute-done.47
  373.8 5.8 %collective-permute-done.63 = bf16[2,384,384]{2,1,0:T(8,128)(2,1)S(1)} collective-permute-done((bf16[2,384,384]{2,1,0:T(8,128)(2,1)S(1)}, bf16[2,384,384]{2,1,0:T(8,128)(2,1)S(1)}, u32[]{:S(2)}, u32[]{:S(2)}) %collective-permute-start.63) | collective-permute-done | bytes 589856 | tf_op jit(solution)/shard_map/ppermute | solution.py:838
  384.7 10.7 %collective-permute-done.56 = bf16[2,48,3840]{2,1,0:T(8,128)(2,1)S(1)} collective-permute-done((bf16[2,48,3840]{2,1,0:T(8,128)(2,1)S(1)}, bf16[2,48,3840]{2,1,0:T(8,128)(2,1)S(1)}, u32[]{:S(2)}, u32[]{:S(2)}) %collective-permute-start.56) | collective-permute-done | bytes 737312 | tf_op jit(solution)/shard_map/ppermute | solution.py:838
  408.8 17.8 %collective-permute-done.67 = bf16[768,384]{1,0:T(8,128)(2,1)S(1)} collective-permute-done((bf16[768,384]{1,0:T(8,128)(2,1)S(1)}, bf16[768,384]{1,0:T(8,128)(2,1)S(1)}, u32[]{:S(2)}, u32[]{:S(2)}) %collective-permute-start.67) | collective-permute-done | bytes 589856 | tf_op jit(solution)/shard_map/ppermute | solution.py:885
  426.9 11.6 %collective-permute-done.60 = bf16[96,3840]{1,0:T(8,128)(2,1)S(1)} collective-permute-done((bf16[96,3840]{1,0:T(8,128)(2,1)S(1)}, bf16[96,3840]{1,0:T(8,128)(2,1)S(1)}, u32[]{:S(2)}, u32[]{:S(2)}) %collective-permute-start.60) | collective-permute-done | bytes 737312 | tf_op jit(solution)/shard_map/ppermute | solution.py:885
  438.9 29.1 %collective-permute-done.68 = bf16[768,384]{1,0:T(8,128)(2,1)S(1)} collective-permute-done((bf16[768,384]{1,0:T(8,128)(2,1)S(1)}, bf16[768,384]{1,0:T(8,128)(2,1)S(1)}, u32[]{:S(2)}, u32[]{:S(2)}) %collective-permute-start.68) | collective-permute-done | bytes 589856 | tf_op jit(solution)/shard_map/ppermute | solution.py:885
  469.5 7.5 %collective-permute-done.61 = bf16[96,3840]{1,0:T(8,128)(2,1)S(1)} collective-permute-done((bf16[96,3840]{1,0:T(8,128)(2,1)S(1)}, bf16[96,3840]{1,0:T(8,128)(2,1)S(1)}, u32[]{:S(2)}, u32[]{:S(2)}) %collective-permute-start.61) | collective-permute-done | bytes 737312 | tf_op jit(solution)/shard_map/ppermute | solution.py:885
  (293 shorter events, 112.5 us)
Async XLA Ops:
  0.7 22.6 %collective-permute-start.9 = (bf16[96,768]{1,0:T(8,128)(2,1)}, bf16[96,768]{1,0:T(8,128)(2,1)S(1)}, u32[]{:S(2)}, u32[]{:S(2)}) collective-permute-start(bf16[96,768]{1,0:T(8,128)(2,1)} %rest_20_.1), channel_id=1, source_target_pairs={{0,8},{4,12},{8,0},{12,4},{16,24},{20,28},{24,16},{28,20},{1,9},{5... | collective-permute-start | bytes 442376 | tf_op jit(solution)/shard_map/ppermute | solution.py:838
  5.2 24.2 %collective-permute-start.13 = (bf16[96,768]{1,0:T(8,128)(2,1)}, bf16[96,768]{1,0:T(8,128)(2,1)S(1)}, u32[]{:S(2)}, u32[]{:S(2)}) collective-permute-start(bf16[96,768]{1,0:T(8,128)(2,1)} %rest_20_.1), channel_id=1, source_target_pairs={{0,4},{4,0},{8,12},{12,8},{16,20},{20,16},{24,28},{28,24},{1,5},{5... | collective-permute-start | bytes 442376 | tf_op jit(solution)/shard_map/ppermute | solution.py:838
  5.2 39.7 %collective-permute-start = (bf16[96,2304]{1,0:T(8,128)(2,1)}, bf16[96,2304]{1,0:T(8,128)(2,1)}, u32[]{:S(2)}, u32[]{:S(2)}) collective-permute-start(bf16[96,2304]{1,0:T(8,128)(2,1)} %rest_2_.1), channel_id=1, source_target_pairs={{0,8},{4,12},{8,0},{12,4},{16,24},{20,28},{24,16},{28,20},{1,9},{5... | collective-permute-start | bytes 1327112 | tf_op jit(solution)/shard_map/ppermute | solution.py:838
  31.5 23.8 %collective-permute-start.19 = (bf16[96,3072]{1,0:T(8,128)(2,1)}, bf16[96,3072]{1,0:T(8,128)(2,1)S(1)}, u32[]{:S(2)}, u32[]{:S(2)}) collective-permute-start(bf16[96,3072]{1,0:T(8,128)(2,1)} %rest_10_.1), channel_id=1, source_target_pairs={{0,16},{4,20},{8,24},{12,28},{16,0},{20,4},{24,8},{28,12},{1,17},{... | collective-permute-start | bytes 1769480 | tf_op jit(solution)/shard_map/ppermute | solution.py:838
  44.8 29.4 %collective-permute-start.22 = (bf16[96,3072]{1,0:T(8,128)(2,1)S(1)}, bf16[96,3072]{1,0:T(8,128)(2,1)}, u32[]{:S(2)}, u32[]{:S(2)}) collective-permute-start(bf16[96,3072]{1,0:T(8,128)(2,1)S(1)} %copy-done.22), channel_id=1, source_target_pairs={{0,4},{4,0},{8,12},{12,8},{16,20},{20,16},{24,28},{28,24},{1,5},{5... | collective-permute-start | bytes 1769480 | tf_op jit(solution)/shard_map/ppermute | solution.py:838
  45.1 29.4 %collective-permute-start.27 = (bf16[384,768]{1,0:T(8,128)(2,1)}, bf16[384,768]{1,0:T(8,128)(2,1)S(1)}, u32[]{:S(2)}, u32[]{:S(2)}) collective-permute-start(bf16[384,768]{1,0:T(8,128)(2,1)} %rest_0_.7), channel_id=1, source_target_pairs={{0,8},{4,12},{8,0},{12,4},{16,24},{20,28},{24,16},{28,20},{1,9},{5... | collective-permute-start | bytes 1769480 | tf_op jit(solution)/shard_map/ppermute | solution.py:838
  45.7 29.9 %collective-permute-start.28 = (bf16[384,768]{1,0:T(8,128)(2,1)}, bf16[384,768]{1,0:T(8,128)(2,1)S(1)}, u32[]{:S(2)}, u32[]{:S(2)}) collective-permute-start(bf16[384,768]{1,0:T(8,128)(2,1)} %rest_0_.7), channel_id=1, source_target_pairs={{0,16},{4,20},{8,24},{12,28},{16,0},{20,4},{24,8},{28,12},{1,17},{... | collective-permute-start | bytes 1769480 | tf_op jit(solution)/shard_map/ppermute | solution.py:838
  49.1 23.1 %collective-permute-start.2 = (bf16[48,2304]{1,0:T(8,128)(2,1)S(1)}, bf16[48,2304]{1,0:T(8,128)(2,1)S(1)}, u32[]{:S(2)}, u32[]{:S(2)}) collective-permute-start(bf16[48,2304]{1,0:T(8,128)(2,1)S(1)} %slice.466), channel_id=1, source_target_pairs={{0,16},{4,20},{8,24},{12,28},{16,0},{20,4},{24,8},{28,12},{1,17},{... | collective-permute-start | bytes 663560 | tf_op jit(solution)/shard_map/ppermute | solution.py:838
  74.3 24.4 %collective-permute-start.5 = (bf16[96,2304]{1,0:T(8,128)(2,1)}, bf16[96,2304]{1,0:T(8,128)(2,1)}, u32[]{:S(2)}, u32[]{:S(2)}) collective-permute-start(bf16[96,2304]{1,0:T(8,128)(2,1)} %collective-permute-done.rest_1_.rest_3_), channel_id=1, source_target_pairs={{0,4},{4,0},{8,12},{12,8},{16,20},{20,16},{24,28},{28,24},{1,5},{5... | collective-permute-start | bytes 1327112 | tf_op jit(solution)/shard_map/ppermute | solution.py:838
  74.4 24.8 %collective-permute-start.6 = (bf16[96,2304]{1,0:T(8,128)(2,1)}, bf16[96,2304]{1,0:T(8,128)(2,1)}, u32[]{:S(2)}, u32[]{:S(2)}) collective-permute-start(bf16[96,2304]{1,0:T(8,128)(2,1)} %collective-permute-done.1.rest_2_.rest_4_), channel_id=1, source_target_pairs={{0,4},{4,0},{8,12},{12,8},{16,20},{20,16},{24,28},{28,24},{1,5},{5... | collective-permute-start | bytes 1327112 | tf_op jit(solution)/shard_map/ppermute | solution.py:838
  75.6 23.7 %collective-permute-start.20 = (bf16[48,3072]{1,0:T(8,128)(2,1)S(1)}, bf16[48,3072]{1,0:T(8,128)(2,1)}, u32[]{:S(2)}, u32[]{:S(2)}) collective-permute-start(bf16[48,3072]{1,0:T(8,128)(2,1)S(1)} %slice.471), channel_id=1, source_target_pairs={{0,16},{4,20},{8,24},{12,28},{16,0},{20,4},{24,8},{28,12},{1,17},{... | collective-permute-start | bytes 884744 | tf_op jit(solution)/shard_map/ppermute | solution.py:838
  77.1 22.6 %collective-permute-start.21 = (bf16[48,3072]{1,0:T(8,128)(2,1)S(1)}, bf16[48,3072]{1,0:T(8,128)(2,1)}, u32[]{:S(2)}, u32[]{:S(2)}) collective-permute-start(bf16[48,3072]{1,0:T(8,128)(2,1)S(1)} %slice.472), channel_id=1, source_target_pairs={{0,8},{4,12},{8,0},{12,4},{16,24},{20,28},{24,16},{28,20},{1,9},{5... | collective-permute-start | bytes 884744 | tf_op jit(solution)/shard_map/ppermute | solution.py:838
  77.7 22.2 %collective-permute-start.29 = (bf16[192,768]{1,0:T(8,128)(2,1)S(1)}, bf16[192,768]{1,0:T(8,128)(2,1)}, u32[]{:S(2)}, u32[]{:S(2)}) collective-permute-start(bf16[192,768]{1,0:T(8,128)(2,1)S(1)} %slice.473), channel_id=1, source_target_pairs={{0,16},{4,20},{8,24},{12,28},{16,0},{20,4},{24,8},{28,12},{1,17},{... | collective-permute-start | bytes 884744 | tf_op jit(solution)/shard_map/ppermute | solution.py:838
  98.7 45.3 %collective-permute-start.30 = (bf16[192,768]{1,0:T(8,128)(2,1)S(1)}, bf16[192,768]{1,0:T(8,128)(2,1)}, u32[]{:S(2)}, u32[]{:S(2)}) collective-permute-start(bf16[192,768]{1,0:T(8,128)(2,1)S(1)} %slice.474), channel_id=1, source_target_pairs={{0,8},{4,12},{8,0},{12,4},{16,24},{20,28},{24,16},{28,20},{1,9},{5... | collective-permute-start | bytes 884744 | tf_op jit(solution)/shard_map/ppermute | solution.py:838
  99.3 45.4 %collective-permute-start.23 = (bf16[96,3072]{1,0:T(8,128)(2,1)S(1)}, bf16[96,3072]{1,0:T(8,128)(2,1)}, u32[]{:S(2)}, u32[]{:S(2)}) collective-permute-start(bf16[96,3072]{1,0:T(8,128)(2,1)S(1)} %collective-permute-done.18.rest_1_.rest_11_), channel_id=1, source_target_pairs={{0,4},{4,0},{8,12},{12,8},{16,20},{20,16},{24,28},{28,24},{1,5},{5... | collective-permute-start | bytes 1769480 | tf_op jit(solution)/shard_map/ppermute | solution.py:838
  99.3 45.8 %collective-permute-start.24 = (bf16[96,3072]{1,0:T(8,128)(2,1)S(1)}, bf16[96,3072]{1,0:T(8,128)(2,1)S(1)}, u32[]{:S(2)}, u32[]{:S(2)}) collective-permute-start(bf16[96,3072]{1,0:T(8,128)(2,1)S(1)} %collective-permute-done.19.rest_2_.rest_12_), channel_id=1, source_target_pairs={{0,4},{4,0},{8,12},{12,8},{16,20},{20,16},{24,28},{28,24},{1,5},{5... | collective-permute-start | bytes 1769480 | tf_op jit(solution)/shard_map/ppermute | solution.py:838
  99.8 44.3 %collective-permute-start.25 = (bf16[48,3072]{1,0:T(8,128)(2,1)}, bf16[48,3072]{1,0:T(8,128)(2,1)}, u32[]{:S(2)}, u32[]{:S(2)}) collective-permute-start(bf16[48,3072]{1,0:T(8,128)(2,1)} %collective-permute-done.20.rest_3_.rest_13_), channel_id=1, source_target_pairs={{0,4},{4,0},{8,12},{12,8},{16,20},{20,16},{24,28},{28,24},{1,5},{5... | collective-permute-start | bytes 884744 | tf_op jit(solution)/shard_map/ppermute | solution.py:838
  99.9 44.7 %collective-permute-start.26 = (bf16[48,3072]{1,0:T(8,128)(2,1)}, bf16[48,3072]{1,0:T(8,128)(2,1)}, u32[]{:S(2)}, u32[]{:S(2)}) collective-permute-start(bf16[48,3072]{1,0:T(8,128)(2,1)} %collective-permute-done.21.rest_4_.rest_14_), channel_id=1, source_target_pairs={{0,4},{4,0},{8,12},{12,8},{16,20},{20,16},{24,28},{28,24},{1,5},{5... | collective-permute-start | bytes 884744 | tf_op jit(solution)/shard_map/ppermute | solution.py:838
  144.0 22.2 %collective-permute-start.31 = (bf16[384,768]{1,0:T(8,128)(2,1)}, bf16[384,768]{1,0:T(8,128)(2,1)S(1)}, u32[]{:S(2)}, u32[]{:S(2)}) collective-permute-start(bf16[384,768]{1,0:T(8,128)(2,1)} %rest_0_.7), channel_id=1, source_target_pairs={{0,4},{4,0},{8,12},{12,8},{16,20},{20,16},{24,28},{28,24},{1,5},{5... | collective-permute-start | bytes 1769480 | tf_op jit(solution)/shard_map/ppermute | solution.py:838
  144.1 22.1 %collective-permute-start.32 = (bf16[384,768]{1,0:T(8,128)(2,1)S(1)}, bf16[384,768]{1,0:T(8,128)(2,1)}, u32[]{:S(2)}, u32[]{:S(2)}) collective-permute-start(bf16[384,768]{1,0:T(8,128)(2,1)S(1)} %collective-permute-done.27.rest_1_), channel_id=1, source_target_pairs={{0,4},{4,0},{8,12},{12,8},{16,20},{20,16},{24,28},{28,24},{1,5},{5... | collective-permute-start | bytes 1769480 | tf_op jit(solution)/shard_map/ppermute | solution.py:838
  144.6 21.7 %collective-permute-start.33 = (bf16[384,768]{1,0:T(8,128)(2,1)S(1)}, bf16[384,768]{1,0:T(8,128)(2,1)}, u32[]{:S(2)}, u32[]{:S(2)}) collective-permute-start(bf16[384,768]{1,0:T(8,128)(2,1)S(1)} %collective-permute-done.28.rest_2_), channel_id=1, source_target_pairs={{0,4},{4,0},{8,12},{12,8},{16,20},{20,16},{24,28},{28,24},{1,5},{5... | collective-permute-start | bytes 1769480 | tf_op jit(solution)/shard_map/ppermute | solution.py:838
  144.7 21.5 %collective-permute-start.34 = (bf16[192,768]{1,0:T(8,128)(2,1)}, bf16[192,768]{1,0:T(8,128)(2,1)S(1)}, u32[]{:S(2)}, u32[]{:S(2)}) collective-permute-start(bf16[192,768]{1,0:T(8,128)(2,1)} %collective-permute-done.29.rest_3_), channel_id=1, source_target_pairs={{0,4},{4,0},{8,12},{12,8},{16,20},{20,16},{24,28},{28,24},{1,5},{5... | collective-permute-start | bytes 884744 | tf_op jit(solution)/shard_map/ppermute | solution.py:838
  145.1 21.1 %collective-permute-start.35 = (bf16[192,768]{1,0:T(8,128)(2,1)}, bf16[192,768]{1,0:T(8,128)(2,1)S(1)}, u32[]{:S(2)}, u32[]{:S(2)}) collective-permute-start(bf16[192,768]{1,0:T(8,128)(2,1)} %collective-permute-done.30.rest_4_), channel_id=1, source_target_pairs={{0,4},{4,0},{8,12},{12,8},{16,20},{20,16},{24,28},{28,24},{1,5},{5... | collective-permute-start | bytes 884744 | tf_op jit(solution)/shard_map/ppermute | solution.py:838
  302.1 23.9 %collective-permute-start.48 = (bf16[4,96,768]{2,1,0:T(8,128)(2,1)}, bf16[4,96,768]{2,1,0:T(8,128)(2,1)S(1)}, u32[]{:S(2)}, u32[]{:S(2)}) collective-permute-start(bf16[4,96,768]{2,1,0:T(8,128)(2,1)} %grad_rows.9), channel_id=1, source_target_pairs={{0,4},{4,0},{8,12},{12,8},{16,20},{20,16},{24,28},{28,24},{1,5},{5... | collective-permute-start | bytes 1769480 | tf_op jit(solution)/shard_map/ppermute | solution.py:838
  319.5 42.0 %collective-permute-start.62 = (bf16[4,768,384]{2,1,0:T(8,128)(2,1)}, bf16[4,768,384]{2,1,0:T(8,128)(2,1)}, u32[]{:S(2)}, u32[]{:S(2)}) collective-permute-start(bf16[4,768,384]{2,1,0:T(8,128)(2,1)} %grad_columns.3), channel_id=1, source_target_pairs={{0,4},{4,0},{8,12},{12,8},{16,20},{20,16},{24,28},{28,24},{1,5},{5... | collective-permute-start | bytes 7077896 | tf_op jit(solution)/shard_map/ppermute | solution.py:838
  319.6 45.7 %collective-permute-start.55 = (bf16[4,96,3840]{2,1,0:T(8,128)(2,1)}, bf16[4,96,3840]{2,1,0:T(8,128)(2,1)}, u32[]{:S(2)}, u32[]{:S(2)}) collective-permute-start(bf16[4,96,3840]{2,1,0:T(8,128)(2,1)} %grad_rows.11), channel_id=1, source_target_pairs={{0,4},{4,0},{8,12},{12,8},{16,20},{20,16},{24,28},{28,24},{1,5},{5... | collective-permute-start | bytes 8847368 | tf_op jit(solution)/shard_map/ppermute | solution.py:838
  367.0 28.3 %collective-permute-start.56 = (bf16[2,48,3840]{2,1,0:T(8,128)(2,1)S(1)}, bf16[2,48,3840]{2,1,0:T(8,128)(2,1)S(1)}, u32[]{:S(2)}, u32[]{:S(2)}) collective-permute-start(bf16[2,48,3840]{2,1,0:T(8,128)(2,1)S(1)} %get-tuple-element.158), channel_id=1, source_target_pairs={{0,8},{4,12},{8,0},{12,4},{16,24},{20,28},{24,16},{28,20},{1,9},{5... | collective-permute-start | bytes 2211848 | tf_op jit(solution)/shard_map/ppermute | solution.py:838
  368.8 28.3 %collective-permute-start.58 = (bf16[2,48,3840]{2,1,0:T(8,128)(2,1)S(1)}, bf16[2,48,3840]{2,1,0:T(8,128)(2,1)S(1)}, u32[]{:S(2)}, u32[]{:S(2)}) collective-permute-start(bf16[2,48,3840]{2,1,0:T(8,128)(2,1)S(1)} %get-tuple-element.159), channel_id=1, source_target_pairs={{0,16},{4,20},{8,24},{12,28},{16,0},{20,4},{24,8},{28,12},{1,17},{... | collective-permute-start | bytes 2211848 | tf_op jit(solution)/shard_map/ppermute | solution.py:838
  404.0 22.6 %collective-permute-start.67 = (bf16[768,384]{1,0:T(8,128)(2,1)S(1)}, bf16[768,384]{1,0:T(8,128)(2,1)S(1)}, u32[]{:S(2)}, u32[]{:S(2)}) collective-permute-start(bf16[768,384]{1,0:T(8,128)(2,1)S(1)} %pad_maximum_fusion.2), channel_id=1, source_target_pairs={{0,1},{1,0},{2,3},{3,2},{4,5},{5,4},{6,7},{7,6},{8,9},{9,8},{10,11... | collective-permute-start | bytes 1769480 | tf_op jit(solution)/shard_map/ppermute | solution.py:885
  408.1 30.3 %collective-permute-start.60 = (bf16[96,3840]{1,0:T(8,128)(2,1)S(1)}, bf16[96,3840]{1,0:T(8,128)(2,1)S(1)}, u32[]{:S(2)}, u32[]{:S(2)}) collective-permute-start(bf16[96,3840]{1,0:T(8,128)(2,1)S(1)} %pad_maximum_fusion.1), channel_id=1, source_target_pairs={{0,1},{1,0},{2,3},{3,2},{4,5},{5,4},{6,7},{7,6},{8,9},{9,8},{10,11... | collective-permute-start | bytes 2211848 | tf_op jit(solution)/shard_map/ppermute | solution.py:885
  426.8 41.2 %collective-permute-start.68 = (bf16[768,384]{1,0:T(8,128)(2,1)S(1)}, bf16[768,384]{1,0:T(8,128)(2,1)S(1)}, u32[]{:S(2)}, u32[]{:S(2)}) collective-permute-start(bf16[768,384]{1,0:T(8,128)(2,1)S(1)} %add_convert_fusion.3), channel_id=1, source_target_pairs={{0,2},{1,3},{2,0},{3,1},{4,6},{5,7},{6,4},{7,5},{8,10},{9,11},{10,... | collective-permute-start | bytes 1769480 | tf_op jit(solution)/shard_map/ppermute | solution.py:885
  438.6 38.5 %collective-permute-start.61 = (bf16[96,3840]{1,0:T(8,128)(2,1)S(1)}, bf16[96,3840]{1,0:T(8,128)(2,1)S(1)}, u32[]{:S(2)}, u32[]{:S(2)}) collective-permute-start(bf16[96,3840]{1,0:T(8,128)(2,1)S(1)} %add_convert_fusion), channel_id=1, source_target_pairs={{0,2},{1,3},{2,0},{3,1},{4,6},{5,7},{6,4},{7,5},{8,10},{9,11},{10,... | collective-permute-start | bytes 2211848 | tf_op jit(solution)/shard_map/ppermute | solution.py:885
  (73 other events, 1006.1 us)
